TPU v7x, 256 devices: a whole 4x4x8 slice. The times are simulated.
256 devices in a mesh: node: 4 (over x), local: 64 (over z, y, core).
Axes of the slice: x: 4, y: 4, z: 8, core: 2. Of those that a mesh axis runs over, the one named last changes fastest.
Arguments:
- query: bfloat16 [32768, 1024], P(('node', 'local')), may hold values from -40 to 40
- key: bfloat16 [32768, 128], P(('node', 'local')), may hold values from -4 to 4
- value: bfloat16 [32768, 128], P(('node', 'local')), may hold values from -6 to 6
- grad_out: bfloat16 [32768, 1024], P(('node', 'local')), may hold values from -6 to 6
- stretch_order: int32 [4, 128], replicated, may hold values from 0 to 127, each once within a row
- reach: int32 [4], replicated, may hold values from 1024 to 2048, as said below
Outputs:
- grad_query: bfloat16 [32768, 1024], P(('node', 'local'))
- grad_key: bfloat16 [32768, 128], P(('node', 'local'))
- grad_value: bfloat16 [32768, 128], P(('node', 'local'))
Inputs may be any that keep to these rules, and one draw needn't show every extreme that they name: `stretch_order`: each row is a permutation of 0 to 127. Some block has reach exactly 2048.
All inputs are finite; a program needn't handle non-finite values.
Results may differ from a plain program's by a relative error of at most 0.04.
Values may be sent and summed in bfloat16 or wider, within the bound.
No kernel may reach another device: no remote copies, remote signals or barrier semaphores. Data moves between devices by JAX's collectives and lax.ppermute only.
A program may use at most 128 MiB of HBM per device.

v0:
```python
import functools

import jax
import jax.numpy as jnp
import numpy as np
from jax import lax
from jax.experimental import pallas as pl
from jax.experimental.pallas import tpu as pltpu
from jax.sharding import PartitionSpec as P

HEAD_DIM = 128
HEADS = 8
STRETCH = 64
SLOTS = 128
BACK = 32
KEYS = BACK + 1
WINDOW = KEYS * STRETCH
COLS = HEADS * STRETCH
CHUNK = 11 * STRETCH
CHUNKS = WINDOW // CHUNK
TAIL = BACK // 2
NZ, NY = 8, 4
LOCAL = NZ * NY * 2
FAR = -1e30

MEMBERS = (((2, 0), (6, 0)), ((1, 2), (5, 2)), ((3, 2), (7, 2)))


def local_of(z, y, c):
    return ((z % NZ) * NY + y % NY) * 2 + c


def moves(by_core):
    out = []
    for source in range(LOCAL):
        z, y, c = source // (NY * 2), (source // 2) % NY, source % 2
        if by_core is None:
            out.append((source, local_of(z, y, 1 - c)))
        else:
            dz, dy = by_core[c]
            out.append((source, local_of(z + dz, y + dy, c)))
    return out


def send(value, by_core):
    return lax.ppermute(value, "local", moves(by_core))


def swap(value):
    return send(value, None)


def shift(value, dz, dy):
    return send(value, ((dz, dy), (dz, dy)))


def gather_block(own, other, unit, send, join, settle=lambda early, late: late):
    swap = functools.partial(send, by_core=None)
    chip = join([own, other])
    first, second, third = [send(chip, by_core=m) for m in MEMBERS]
    opposite = send(first[:unit], by_core=MEMBERS[0])
    mine = join([own, second, settle(first, opposite), first, third])
    half = 4 * unit
    up, down = [send(mine, by_core=((0, dy), (0, dy))) for dy in (1, -1)]
    ahead, behind = [send(mine[:half], by_core=((dz, 0), (dz, 0))) for dz in (1, -1)]
    pieces = [mine, up, down, ahead, behind]
    return pieces + [swap(piece) for piece in pieces]


def piece_table():
    labels = np.arange(SLOTS).reshape(LOCAL, 2).T

    def fake_send(value, by_core):
        out = np.empty_like(value)
        for source, target in moves(by_core):
            out[:, target] = value[:, source]
        return out

    pieces = gather_block(labels, fake_send(labels, None), 2, fake_send, lambda parts: np.concatenate(parts, 0))
    order = np.concatenate(pieces, 0).T
    table = np.empty((LOCAL, SLOTS), np.int32)
    for device in range(LOCAL):
        table[device, order[device]] = np.arange(SLOTS)
    return table


TABLE = piece_table()
PIECES = (16, 16, 16, 8, 8) * 2
ALL = PIECES + (TAIL, TAIL)
STARTS = tuple(int(s) for s in np.cumsum((0,) + ALL))
KEY_COST = 0
VALUE_COST = 6
VMEM_LIMIT = 36 * 2**20
PICK_KIB = 12 * 1024
MERGE_KIB = 16 * 1024

SMEM = pl.BlockSpec(memory_space=pltpu.SMEM)
VMEM = pl.BlockSpec(memory_space=pltpu.VMEM)


def at(i, size=STRETCH):
    return pl.ds(pl.multiple_of(i * size, size), size)


def shape(rows, columns=HEAD_DIM, dtype=jnp.bfloat16):
    return jax.ShapeDtypeStruct((rows, columns), dtype)


def lay(refs, held, columns=slice(None)):
    first = 0
    for ref in refs:
        held[pl.ds(first, ref.shape[0])] = ref[:, columns]
        first += ref.shape[0]


def small(kib):
    return pltpu.CompilerParams(vmem_limit_bytes=kib * 1024)


def plan_kernel(order, reach, table, places, tail_places, facts, inverse):
    node, local = lax.axis_index("node"), lax.axis_index("local")
    core = local % 2

    def turn(s, carry):
        inverse[order[node, s]] = table[local, s]
        return carry

    lax.fori_loop(0, SLOTS, turn, 0, unroll=8)
    for i in range(TAIL):
        tail_places[i] = inverse[SLOTS - BACK + core * TAIL + i]
    facts[4] = reach[node]
    for c in range(2):
        own = order[node, 2 * local + c]
        facts[c] = own
        first = jnp.where(node > 0, 0, jnp.maximum(BACK - own, 0))
        facts[2 + c] = first

        def find(k, carry, c=c, own=own):
            wanted = own - BACK + k
            tail = jnp.maximum(wanted + BACK, 0)
            half = tail // TAIL
            in_tail = SLOTS + jnp.where(half == core, 0, TAIL) + tail % TAIL
            now = inverse[jnp.maximum(wanted, 0)]
            places[c * KEYS + k] = jnp.where(wanted >= 0, now, jnp.where(node > 0, in_tail, 0))
            return carry

        lax.fori_loop(0, KEYS, find, 0, unroll=3)


def plan(stretch_order, reach):
    return pl.pallas_call(
        plan_kernel,
        out_shape=tuple(jax.ShapeDtypeStruct((n,), jnp.int32) for n in (2 * KEYS, TAIL, 5)),
        in_specs=[SMEM] * 3,
        out_specs=(SMEM,) * 3,
        scratch_shapes=[pltpu.SMEM((SLOTS,), jnp.int32)],
        compiler_params=small(256),
        name="plan",
    )(stretch_order, reach, jnp.asarray(TABLE))


def pick_kernel(places, *refs):
    pieces, keys, values, held = refs[: len(PIECES)], *refs[len(PIECES) :]
    lay(pieces, held)

    def one(i, carry):
        rows = held[at(places[i])]
        keys[at(i)], values[at(i)] = rows[:, :HEAD_DIM], rows[:, HEAD_DIM:]
        return carry

    lax.fori_loop(0, TAIL, one, 0)


def pick(places, pieces):
    return pl.pallas_call(
        pick_kernel,
        out_shape=(shape(TAIL * STRETCH),) * 2,
        in_specs=[SMEM] + [VMEM] * len(pieces),
        out_specs=(VMEM,) * 2,
        scratch_shapes=[pltpu.VMEM((SLOTS * STRETCH, 2 * HEAD_DIM), jnp.bfloat16)],
        compiler_params=small(PICK_KIB),
        name="pick_tail",
    )(places, *pieces)


def stack_heads(array, heads):
    for c in range(2):
        for h in range(HEADS):
            heads[c, pl.ds(h * STRETCH, STRETCH)] = array[
                pl.ds(c * STRETCH, STRETCH), pl.ds(h * HEAD_DIM, HEAD_DIM)
            ]


def fetch(places, c, held, window):
    def one(k, carry):
        window[at(k)] = held[at(places[c * KEYS + k])]
        return carry

    lax.fori_loop(0, KEYS, one, 0, unroll=11)


def spread(places, facts, terms, held):
    def clear(i, carry):
        held[at(i, 256)] = jnp.zeros((256, HEAD_DIM), jnp.bfloat16)
        return carry

    lax.fori_loop(0, held.shape[0] // 256, clear, 0, unroll=8)

    dump = SLOTS + BACK

    def first(k, carry):
        place = jnp.where(k >= facts[2], places[k], dump)
        held[at(place)] = terms[0, at(k)].astype(jnp.bfloat16)
        return carry

    lax.fori_loop(0, KEYS, first, 0, unroll=11)

    def second(k, carry):
        place = jnp.where(k >= facts[3], places[KEYS + k], dump)
        twin = k + facts[1] - facts[0]
        both = (twin >= facts[2]) & (twin < KEYS)
        twin = jnp.clip(twin, 0, KEYS - 1)
        term = terms[1, at(k)] + jnp.where(both, terms[0, at(twin)], 0.0)
        held[at(place)] = term.astype(jnp.bfloat16)
        return carry

    lax.fori_loop(0, KEYS, second, 0, unroll=11)


def give(held, outs, first=0):
    for out in outs:
        out[...] = held[pl.ds(first, out.shape[0])]
        first += out.shape[0]


def dot(a, b, over):
    return lax.dot_general(a, b, ((over[:1], over[1:]), ((), ())), preferred_element_type=jnp.float32)


def key_kernel(places, facts, query, grad_out, *refs):
    pieces, refs = refs[: len(ALL)], refs[len(ALL) :]
    prob_out, keys_out, q_heads, g_heads, held, *outs = refs[:7]
    score, terms = refs[7:]
    lay(pieces, held, pl.ds(0, HEAD_DIM))
    scale = 1.4426950408889634 / HEAD_DIM**0.5
    stack_heads(query, q_heads)
    stack_heads(grad_out, g_heads)
    token = lax.broadcasted_iota(jnp.int32, (1, COLS), 1) % STRETCH
    latest = BACK * STRETCH + token

    def stretch(c, carry):
        window = keys_out.at[c]
        fetch(places, c, held, window)
        q, g = q_heads[c], g_heads[c]
        earliest = jnp.maximum(latest - facts[4], facts[2 + c] * STRETCH)
        peaks, totals = [], []
        for j in range(CHUNKS):
            rows = pl.ds(j * CHUNK, CHUNK)
            raw = dot(window[rows], q, (1, 1))
            row = lax.broadcasted_iota(jnp.int32, (CHUNK, COLS), 0) + j * CHUNK
            seen = row >= earliest
            if (j + 1) * CHUNK > BACK * STRETCH:
                seen = seen & (row <= latest)
            raw = jnp.where(seen, raw * scale, FAR)
            score[c, rows] = raw
            peaks.append(jnp.max(raw, axis=0, keepdims=True))
            expd = jnp.exp2(score[c, rows] - peaks[j])
            score[c, rows] = expd
            totals.append(jnp.sum(expd, axis=0, keepdims=True))
        peak = functools.reduce(jnp.maximum, peaks)
        weights = [jnp.exp2(p - peak) for p in peaks]
        share = 1.0 / sum(w * t for w, t in zip(weights, totals))
        for j in range(CHUNKS):
            rows = pl.ds(j * CHUNK, CHUNK)
            prob = (score[c, rows] * (share * weights[j])).astype(jnp.bfloat16)
            prob_out[c, rows] = prob
            terms[c, rows] = dot(prob, g, (1, 0))
        return carry

    lax.fori_loop(0, 2, stretch, 0)
    spread(places, facts, terms, held)
    give(held, outs, SLOTS * STRETCH)


def value_kernel(places, facts, prob_in, keys_in, q_heads, g_heads, *refs):
    pieces, refs = refs[: len(ALL)], refs[len(ALL) :]
    grad_query, held, *outs = refs[:4]
    window, dprob, terms = refs[4:]
    lay(pieces[: len(PIECES)], held, pl.ds(HEAD_DIM, HEAD_DIM))
    lay(pieces[len(PIECES) :], held.at[pl.ds(SLOTS * STRETCH, 2 * TAIL * STRETCH)])
    scale = 1.0 / HEAD_DIM**0.5

    def stretch(c, carry):
        fetch(places, c, held, window.at[c])
        q, g = q_heads[c], g_heads[c]
        delta = 0.0
        for j in range(CHUNKS):
            rows = pl.ds(j * CHUNK, CHUNK)
            dp = dot(window[c, rows], g, (1, 1))
            dprob[c, rows] = dp
            delta = delta + jnp.sum(prob_in[c, rows].astype(jnp.float32) * dp, axis=0, keepdims=True)
        dq = 0.0
        for j in range(CHUNKS):
            rows = pl.ds(j * CHUNK, CHUNK)
            prob = prob_in[c, rows].astype(jnp.float32)
            dscore = (prob * (dprob[c, rows] - delta)).astype(jnp.bfloat16)
            terms[c, rows] = dot(dscore, q, (1, 0)) * scale
            dq = dq + dot(keys_in[c, rows], dscore, (0, 0))
        dq = (jnp.transpose(dq) * scale).astype(jnp.bfloat16)
        for h in range(HEADS):
            grad_query[at(c), pl.ds(h * HEAD_DIM, HEAD_DIM)] = dq[
                h * STRETCH : (h + 1) * STRETCH
            ]
        return carry

    lax.fori_loop(0, 2, stretch, 0)
    spread(places, facts, terms, held)
    give(held, outs, SLOTS * STRETCH)


PIECE_SHAPES = tuple(shape(n * STRETCH, 2 * HEAD_DIM) for n in PIECES)
TERM_SHAPES = (shape((SLOTS + BACK + 1) * STRETCH), shape(TAIL * STRETCH), shape(TAIL * STRETCH))
HEAD_SHAPE = jax.ShapeDtypeStruct((2, COLS, HEAD_DIM), jnp.bfloat16)


def cost(matmuls):
    return pl.CostEstimate(
        flops=matmuls * 4 * WINDOW * COLS * HEAD_DIM, bytes_accessed=matmuls * 2**21, transcendentals=0
    )


def on_keys(places, facts, query, grad_out, pieces):
    return pl.pallas_call(
        key_kernel,
        out_shape=(
            jax.ShapeDtypeStruct((2, WINDOW, COLS), jnp.bfloat16),
            jax.ShapeDtypeStruct((2, WINDOW, HEAD_DIM), jnp.bfloat16),
            HEAD_SHAPE,
            HEAD_SHAPE,
        )
        + TERM_SHAPES,
        in_specs=[SMEM, SMEM] + [VMEM] * (2 + len(pieces)),
        out_specs=(VMEM,) * 7,
        scratch_shapes=[
            pltpu.VMEM((2, WINDOW, COLS), jnp.float32),
            pltpu.VMEM((2, WINDOW, HEAD_DIM), jnp.float32),
        ],
        compiler_params=pltpu.CompilerParams(vmem_limit_bytes=VMEM_LIMIT),
        cost_estimate=cost(KEY_COST),
        name="on_keys",
    )(places, facts, query, grad_out, *pieces)


def on_values(places, facts, carried, pieces):
    return pl.pallas_call(
        value_kernel,
        out_shape=(shape(2 * STRETCH, HEADS * HEAD_DIM),) + TERM_SHAPES,
        in_specs=[SMEM, SMEM] + [VMEM] * (4 + len(pieces)),
        out_specs=(VMEM,) * 4,
        scratch_shapes=[
            pltpu.VMEM((2, WINDOW, HEAD_DIM), jnp.bfloat16),
            pltpu.VMEM((2, WINDOW, COLS), jnp.float32),
            pltpu.VMEM((2, WINDOW, HEAD_DIM), jnp.float32),
        ],
        compiler_params=pltpu.CompilerParams(vmem_limit_bytes=VMEM_LIMIT),
        cost_estimate=cost(VALUE_COST),
        name="on_values",
    )(places, facts, *carried, *pieces)


def merge_kernel(places, keys, values, tail_keys, tail_values, *refs):
    outs, held = refs[:-1], refs[-1]
    for i, (block, tail) in enumerate(((keys, tail_keys), (values, tail_values))):
        columns = pl.ds(i * HEAD_DIM, HEAD_DIM)
        held[:, columns] = block[: SLOTS * STRETCH]

        def one(j, carry, tail=tail, columns=columns):
            rows = at(places[j])
            total = held[rows, columns].astype(jnp.float32) + tail[at(j)].astype(jnp.float32)
            held[rows, columns] = total.astype(jnp.bfloat16)
            return carry

        lax.fori_loop(0, TAIL, one, 0)
    give(held, outs)


def merge(places, *arrays):
    return pl.pallas_call(
        merge_kernel,
        out_shape=PIECE_SHAPES,
        in_specs=[SMEM] + [VMEM] * len(arrays),
        out_specs=(VMEM,) * len(PIECES),
        scratch_shapes=[pltpu.VMEM((SLOTS * STRETCH, 2 * HEAD_DIM), jnp.bfloat16)],
        compiler_params=small(MERGE_KIB),
        name="merge_tail",
    )(places, *arrays)


def join(parts):
    return jnp.concatenate(parts, 0)


def wide(value):
    return value.astype(jnp.float32)


def reduce_block(pieces, unit):
    own, other = pieces[:5], pieces[5:]
    arrived = [swap(piece) for piece in other]
    sums = [wide(a) + wide(b) for a, b in zip(own, arrived)]
    mine, up, down, ahead, behind = [sums[0]] + [s.astype(jnp.bfloat16) for s in sums[1:]]
    up, down = shift(up, 0, -1), shift(down, 0, 1)
    ahead, behind = shift(ahead, -1, 0), shift(behind, 1, 0)
    half = ahead.shape[0]
    mine = mine + wide(up) + wide(down)
    mine = jnp.concatenate([mine[:half] + wide(ahead) + wide(behind), mine[half:]], 0)
    mine_b = mine.astype(jnp.bfloat16)
    home = [tuple((-dz, -dy) for dz, dy in m) for m in MEMBERS]
    first = send(mine_b[3 * unit : 6 * unit], home[0])
    second, third = send(mine_b[unit : 3 * unit], home[1]), send(mine_b[6 * unit :], home[2])
    opposite = send(first[:unit], home[0])
    there = wide(first[2 * unit :]) + wide(second[unit:]) + wide(third[unit:])
    here = mine[:unit] + wide(opposite) + wide(first[unit : 2 * unit]) + wide(second[:unit]) + wide(third[:unit])
    return here + wide(swap(there.astype(jnp.bfloat16)))


def per_device(query, key, value, grad_out, stretch_order, reach):
    unit = query.shape[0]
    nodes = lax.axis_size("node")
    onward = [(n, (n + 1) % nodes) for n in range(nodes)]
    backward = [((n + 1) % nodes, n) for n in range(nodes)]
    tables = []

    def settle(early, late):
        tables.extend(plan(stretch_order, lax.optimization_barrier((reach, early))[0]))
        late, *tables[:] = lax.optimization_barrier((late, *tables))
        return late

    own, other = [jnp.concatenate(rows, axis=1) for rows in ((key, value), (swap(key), swap(value)))]
    pieces = gather_block(own, other, unit, send, join, settle)
    places, tail_places, facts = tables
    tails = [lax.ppermute(tail, "node", onward) for tail in pick(tail_places, pieces)]
    keys, values = [pieces + [tail, swap(tail)] for tail in tails]

    *carried, block_values, own_tail, other_tail = on_keys(places, facts, query, grad_out, keys)
    tail_values = (wide(own_tail) + wide(swap(other_tail))).astype(jnp.bfloat16)
    carried[0], tail_values = lax.optimization_barrier((carried[0], tail_values))
    tail_values = lax.ppermute(tail_values, "node", backward)
    grad_query, block_keys, own_tail, other_tail = on_values(places, facts, carried, values)
    tail_values, own_tail, other_tail = lax.optimization_barrier((tail_values, own_tail, other_tail))
    tail_keys = (wide(own_tail) + wide(swap(other_tail))).astype(jnp.bfloat16)
    tail_keys = lax.ppermute(tail_keys, "node", backward)
    pieces = merge(tail_places, block_keys, block_values, tail_keys, tail_values)
    sums = reduce_block(pieces, unit).astype(jnp.bfloat16)
    return grad_query, sums[:, :HEAD_DIM], sums[:, HEAD_DIM:]


def solution(mesh):
    rows = P(("node", "local"), None)
    return jax.shard_map(
        per_device,
        mesh=mesh,
        in_specs=(rows, rows, rows, rows, P(), P()),
        out_specs=(rows, rows, rows),
        check_vma=False,
    )
```

profile of v0, /device:TPU:6, one launch (start us, length us, event | category | flops | bytes accessed | tf_op | source)
XLA Modules:
  0.0 121.0 jit_solution(9103727019461479298)
XLA Ops:
  0.6 0.1 collective-permute-start
  0.7 0.5 collective-permute-start.1
  1.2 0.8 constant_dynamic-update-slice_fusion.7
  2.0 0.8 constant_dynamic-update-slice_fusion.6
  2.8 3.3 %collective-permute-start.2 = (bf16[256,256]{1,0:T(8,128)(2,1)S(1)}, bf16[256,256]{1,0:T(8,128)(2,1)S(1)}, u32[]{:S(2)}, u32[]{:S(2)}) collective-permute-start(bf16[256,256]{1,0:T(8,128)(2,1)S(1)} %maximum_maximum_fusion), channel_id=1, source_target_pairs={{0,16},{1,49},{2,18},{3,51},{4,20},{5,53},{6,22},{7,55},{8,24},{9,... | collective-permute-start | bytes 393224 | tf_op jit(solution)/shard_map/ppermute | solution.py:46
  6.2 4.5 %collective-permute-start.4 = (bf16[256,256]{1,0:T(8,128)(2,1)S(1)}, bf16[256,256]{1,0:T(8,128)(2,1)S(1)}, u32[]{:S(2)}, u32[]{:S(2)}) collective-permute-start(bf16[256,256]{1,0:T(8,128)(2,1)S(1)} %maximum_maximum_fusion), channel_id=1, source_target_pairs={{0,12},{1,45},{2,14},{3,47},{4,8},{5,41},{6,10},{7,43},{8,20},{9,5... | collective-permute-start | bytes 393224 | tf_op jit(solution)/shard_map/ppermute | solution.py:46
  10.7 3.8 %collective-permute-start.5 = (bf16[256,256]{1,0:T(8,128)(2,1)S(1)}, bf16[256,256]{1,0:T(8,128)(2,1)S(1)}, u32[]{:S(2)}, u32[]{:S(2)}) collective-permute-start(bf16[256,256]{1,0:T(8,128)(2,1)S(1)} %maximum_maximum_fusion), channel_id=1, source_target_pairs={{0,28},{1,61},{2,30},{3,63},{4,24},{5,57},{6,26},{7,59},{8,36},{9,... | collective-permute-start | bytes 393224 | tf_op jit(solution)/shard_map/ppermute | solution.py:46
  14.5 0.8 collective-permute-start.3
  15.3 0.8 copy-done.2
  16.1 0.7 copy-done.3
  16.7 0.7 copy-done.4
  17.4 2.8 %plan.1 = (s32[66]{0:T(128)S(1)}, s32[16]{0:T(128)S(1)}, s32[5]{0:T(128)S(1)}) custom-call(s32[4,128]{1,0:T(4,128)S(1)} %copy-done.3, s32[4]{0:T(128)S(1)} %copy-done.4, s32[64,128]{1,0:T(8,128)S(1)} %copy-done.2), custom_call_target="tpu_custom_call" | custom-call | tf_op jit(solution)/shard_map/plan/pallas_call | solution.py:151
  20.3 2.3 %collective-permute-done.3 = bf16[128,256]{1,0:T(8,128)(2,1)S(1)} collective-permute-done((bf16[128,256]{1,0:T(8,128)(2,1)S(1)}, bf16[128,256]{1,0:T(8,128)(2,1)S(1)}, u32[]{:S(2)}, u32[]{:S(2)}) %collective-permute-start.3) | collective-permute-done | bytes 65568 | tf_op jit(solution)/shard_map/ppermute | solution.py:46
  22.6 0.5 collective-permute-done.5
  23.1 2.3 %collective-permute-start.7 = (bf16[1024,256]{1,0:T(8,128)(2,1)S(1)}, bf16[1024,256]{1,0:T(8,128)(2,1)S(1)}, u32[]{:S(2)}, u32[]{:S(2)}) collective-permute-start(bf16[1024,256]{1,0:T(8,128)(2,1)S(1)} %constant_dynamic-update-slice_fusion.2.refs_0_), channel_id=1, source_target_pairs={{0,6},{1,7},{2,0},{3,1},{4,2},{5,3},{6,4},{7,5},{8,14},{9,15},{10,... | collective-permute-start | bytes 1572872 | tf_op jit(solution)/shard_map/ppermute | solution.py:46
  25.5 1.6 %collective-permute-start.9 = (bf16[512,256]{1,0:T(8,128)(2,1)S(1)}, bf16[512,256]{1,0:T(8,128)(2,1)S(1)}, u32[]{:S(2)}, u32[]{:S(2)}) collective-permute-start(bf16[512,256]{1,0:T(8,128)(2,1)S(1)} %pad_maximum_fusion), channel_id=1, source_target_pairs={{0,56},{1,57},{2,58},{3,59},{4,60},{5,61},{6,62},{7,63},{8,0},{9,1... | collective-permute-start | bytes 786440 | tf_op jit(solution)/shard_map/ppermute | solution.py:46
  27.0 1.2 collective-permute-start.8
  28.2 9.2 %collective-permute-done.7.refs_2_ = bf16[1024,256]{1,0:T(8,128)(2,1)S(1)} collective-permute-done((bf16[1024,256]{1,0:T(8,128)(2,1)S(1)}, bf16[1024,256]{1,0:T(8,128)(2,1)S(1)}, u32[]{:S(2)}, u32[]{:S(2)}) %collective-permute-start.7) | collective-permute-done | bytes 524320 | tf_op jit(solution)/shard_map/ppermute | solution.py:46
  37.4 3.4 %collective-permute-done.6.refs_1_ = bf16[1024,256]{1,0:T(8,128)(2,1)S(1)} collective-permute-done((bf16[1024,256]{1,0:T(8,128)(2,1)S(1)}, bf16[1024,256]{1,0:T(8,128)(2,1)S(1)}, u32[]{:S(2)}, u32[]{:S(2)}) %collective-permute-start.6) | collective-permute-done | bytes 524320 | tf_op jit(solution)/shard_map/ppermute | solution.py:46
  40.9 0.5 collective-permute-start.14
  41.4 0.1 collective-permute-start.13
  41.5 1.7 %collective-permute-done.14.refs_9_ = bf16[512,256]{1,0:T(8,128)(2,1)S(1)} collective-permute-done((bf16[512,256]{1,0:T(8,128)(2,1)S(1)}, bf16[512,256]{1,0:T(8,128)(2,1)S(1)}, u32[]{:S(2)}, u32[]{:S(2)}) %collective-permute-start.14) | collective-permute-done | bytes 262176 | tf_op jit(solution)/shard_map/ppermute | solution.py:46
  43.1 0.4 collective-permute-done.13.refs_8_
  43.5 1.0 pick_tail.1
  44.5 0.6 collective-permute-start.15
  45.1 7.9 %collective-permute-done.15.refs_10_ = bf16[1024,128]{1,0:T(8,128)(2,1)S(1)} collective-permute-done((bf16[1024,128]{1,0:T(8,128)(2,1)S(1)}, bf16[1024,128]{1,0:T(8,128)(2,1)S(1)}, u32[]{:S(2)}, u32[]{:S(2)}) %collective-permute-start.15) | collective-permute-done | bytes 262176 | tf_op jit(solution)/shard_map/ppermute | solution.py:442
  52.9 1.7 %collective-permute-start.18 = (bf16[1024,128]{1,0:T(8,128)(2,1)S(1)}, bf16[1024,128]{1,0:T(8,128)(2,1)S(1)}, u32[]{:S(2)}, u32[]{:S(2)}) collective-permute-start(bf16[1024,128]{1,0:T(8,128)(2,1)S(1)} %get-tuple-element.55), channel_id=1, source_target_pairs={{0,64},{64,128},{128,192},{192,0},{1,65},{65,129},{129,193},{193,1... | collective-permute-start | bytes 786440 | tf_op jit(solution)/shard_map/ppermute | solution.py:442
  54.6 7.2 %on_keys.1 = (bf16[2,2112,512]{2,1,0:T(8,128)(2,1)S(1)}, bf16[2,2112,128]{2,1,0:T(8,128)(2,1)S(1)}, bf16[2,512,128]{2,1,0:T(8,128)(2,1)S(1)}, bf16[2,512,128]{2,...) custom-call(s32[66]{0:T(128)S(1)} %get-tuple-element.43.places, ...), custom_call_target="tpu_custom_call" | custom-call | tf_op jit(solution)/shard_map/on_keys/pallas_call | solution.py:333
  61.8 0.3 collective-permute-start.17
  62.2 0.3 collective-permute-start.19
  62.4 1.0 collective-permute-done.17
  63.5 0.7 collective-permute-start.20
  64.3 6.8 %on_values.1 = (bf16[128,1024]{1,0:T(8,128)(2,1)}, bf16[10304,128]{1,0:T(8,128)(2,1)S(1)}, bf16[1024,128]{1,0:T(8,128)(2,1)S(1)}, bf16[1024,128]{1,0:T(8,128)(2,1)S(1)}) custom-call(s32[66]{0:T(128)S(1)} %get-tuple-element.43.places, s32[5]{0:T(128)S(1)} %get-tuple-element.44.facts, bf16[2,2112,512]{2,1,0:T(8,128)(2,1)S(1)} %get-tuple-element.51.prob_in, ...), custom_call_target="tpu_custom_call" | custom-call | flops 3321888768 | bytes 12582912 | tf_op jit(solution)/shard_map/on_values/pallas_call | solution.py:355
  71.1 2.2 %collective-permute-done.20.tail_values = bf16[1024,128]{1,0:T(8,128)(2,1)S(1)} collective-permute-done((bf16[1024,128]{1,0:T(8,128)(2,1)S(1)}, bf16[1024,128]{1,0:T(8,128)(2,1)S(1)}, u32[]{:S(2)}, u32[]{:S(2)}) %collective-permute-start.20) | collective-permute-done | bytes 262176 | tf_op jit(solution)/shard_map/ppermute | solution.py:448
  73.3 1.5 %collective-permute-done.21 = bf16[1024,128]{1,0:T(8,128)(2,1)S(1)} collective-permute-done((bf16[1024,128]{1,0:T(8,128)(2,1)S(1)}, bf16[1024,128]{1,0:T(8,128)(2,1)S(1)}, u32[]{:S(2)}, u32[]{:S(2)}) %collective-permute-start.21) | collective-permute-done | bytes 262176 | tf_op jit(solution)/shard_map/ppermute | solution.py:46
  75.0 9.5 %collective-permute-done.22.tail_keys = bf16[1024,128]{1,0:T(8,128)(2,1)S(1)} collective-permute-done((bf16[1024,128]{1,0:T(8,128)(2,1)S(1)}, bf16[1024,128]{1,0:T(8,128)(2,1)S(1)}, u32[]{:S(2)}, u32[]{:S(2)}) %collective-permute-start.22) | collective-permute-done | bytes 262176 | tf_op jit(solution)/shard_map/ppermute | solution.py:452
  84.5 1.8 %merge_tail.1 = (bf16[1024,256]{1,0:T(8,128)(2,1)S(1)}, bf16[1024,256]{1,0:T(8,128)(2,1)S(1)}, bf16[1024,256]{1,0:T(8,128)(2,1)S(1)}, bf16[512,256]{1,0:T(8,128)...) custom-call(s32[16]{0:T(128)S(1)} %get-tuple-element.46.places, ...), custom_call_target="tpu_custom_call" | custom-call | tf_op jit(solution)/shard_map/merge_tail/pallas_call | solution.py:388
  86.4 0.1 collective-permute-start.24
  86.5 0.5 collective-permute-start.26
  87.0 0.1 collective-permute-start.28
  87.1 0.4 collective-permute-start.23
  87.5 0.9 collective-permute-done.24
  88.4 0.1 add_convert_fusion.1
  88.5 1.1 collective-permute-start.25
  89.6 0.1 add_convert_fusion
  89.8 1.1 collective-permute-start.27
  90.9 0.1 collective-permute-start.29
  91.0 1.4 %collective-permute-done.30 = bf16[512,256]{1,0:T(8,128)(2,1)S(1)} collective-permute-done((bf16[512,256]{1,0:T(8,128)(2,1)S(1)}, bf16[512,256]{1,0:T(8,128)(2,1)S(1)}, u32[]{:S(2)}, u32[]{:S(2)}) %collective-permute-start.30) | collective-permute-done | bytes 262176 | tf_op jit(solution)/shard_map/ppermute | solution.py:46
  92.5 0.7 collective-permute-start.31
  93.2 9.4 %collective-permute-done.25 = bf16[1024,256]{1,0:T(8,128)(2,1)S(1)} collective-permute-done((bf16[1024,256]{1,0:T(8,128)(2,1)S(1)}, bf16[1024,256]{1,0:T(8,128)(2,1)S(1)}, u32[]{:S(2)}, u32[]{:S(2)}) %collective-permute-start.25) | collective-permute-done | bytes 524320 | tf_op jit(solution)/shard_map/ppermute | solution.py:46
  102.6 2.2 %collective-permute-done.27 = bf16[1024,256]{1,0:T(8,128)(2,1)S(1)} collective-permute-done((bf16[1024,256]{1,0:T(8,128)(2,1)S(1)}, bf16[1024,256]{1,0:T(8,128)(2,1)S(1)}, u32[]{:S(2)}, u32[]{:S(2)}) %collective-permute-start.27) | collective-permute-done | bytes 524320 | tf_op jit(solution)/shard_map/ppermute | solution.py:46
  104.8 0.3 fusion.8
  105.1 0.1 fusion.6
  105.2 1.2 collective-permute-start.32
  106.4 1.7 %collective-permute-start.35 = (bf16[256,256]{1,0:T(8,128)(2,1)S(1)}, bf16[256,256]{1,0:T(8,128)(2,1)S(1)}, u32[]{:S(2)}, u32[]{:S(2)}) collective-permute-start(bf16[256,256]{1,0:T(8,128)(2,1)S(1)} %slice.79), channel_id=1, source_target_pairs={{0,44},{1,13},{2,46},{3,15},{4,40},{5,9},{6,42},{7,11},{8,52},{9,2... | collective-permute-start | bytes 393224 | tf_op jit(solution)/shard_map/ppermute | solution.py:46
  108.1 3.2 %collective-permute-start.34 = (bf16[256,256]{1,0:T(8,128)(2,1)S(1)}, bf16[256,256]{1,0:T(8,128)(2,1)S(1)}, u32[]{:S(2)}, u32[]{:S(2)}) collective-permute-start(bf16[256,256]{1,0:T(8,128)(2,1)S(1)} %slice.77), channel_id=1, source_target_pairs={{0,60},{1,29},{2,62},{3,31},{4,56},{5,25},{6,58},{7,27},{8,4},{9,3... | collective-permute-start | bytes 393224 | tf_op jit(solution)/shard_map/ppermute | solution.py:46
  111.3 2.4 %collective-permute-done.32 = bf16[384,256]{1,0:T(8,128)(2,1)S(1)} collective-permute-done((bf16[384,256]{1,0:T(8,128)(2,1)S(1)}, bf16[384,256]{1,0:T(8,128)(2,1)S(1)}, u32[]{:S(2)}, u32[]{:S(2)}) %collective-permute-start.32) | collective-permute-done | bytes 196640 | tf_op jit(solution)/shard_map/ppermute | solution.py:46
  113.8 2.9 %collective-permute-start.33 = (bf16[128,256]{1,0:T(8,128)(2,1)S(1)}, bf16[128,256]{1,0:T(8,128)(2,1)S(1)}, u32[]{:S(2)}, u32[]{:S(2)}) collective-permute-start(bf16[128,256]{1,0:T(8,128)(2,1)S(1)} %slice.75), channel_id=1, source_target_pairs={{0,48},{1,17},{2,50},{3,19},{4,52},{5,21},{6,54},{7,23},{8,56},{9,... | collective-permute-start | bytes 196616 | tf_op jit(solution)/shard_map/ppermute | solution.py:46
  116.7 0.7 collective-permute-done.35
  117.4 1.2 collective-permute-done.34
  118.6 0.8 collective-permute-start.36
  119.4 0.5 collective-permute-done.33
  119.8 0.4 collective-permute-done.36
  120.3 0.6 fusion.9
  (50 shorter events, 0.7 us)
Async XLA Ops:
  0.6 2.2 %collective-permute-start = (bf16[128,128]{1,0:T(8,128)(2,1)}, bf16[128,128]{1,0:T(8,128)(2,1)S(1)}, u32[]{:S(2)}, u32[]{:S(2)}) collective-permute-start(bf16[128,128]{1,0:T(8,128)(2,1)} %param.8), channel_id=1, source_target_pairs={{0,1},{1,0},{2,3},{3,2},{4,5},{5,4},{6,7},{7,6},{8,9},{9,8},{10,11... | collective-permute-start | bytes 98312 | tf_op jit(solution)/shard_map/ppermute | solution.py:46
  0.7 2.1 %collective-permute-start.1 = (bf16[128,128]{1,0:T(8,128)(2,1)}, bf16[128,128]{1,0:T(8,128)(2,1)S(1)}, u32[]{:S(2)}, u32[]{:S(2)}) collective-permute-start(bf16[128,128]{1,0:T(8,128)(2,1)} %param.9), channel_id=1, source_target_pairs={{0,1},{1,0},{2,3},{3,2},{4,5},{5,4},{6,7},{7,6},{8,9},{9,8},{10,11... | collective-permute-start | bytes 98312 | tf_op jit(solution)/shard_map/ppermute | solution.py:46
  2.8 11.7 %collective-permute-start.2 = (bf16[256,256]{1,0:T(8,128)(2,1)S(1)}, bf16[256,256]{1,0:T(8,128)(2,1)S(1)}, u32[]{:S(2)}, u32[]{:S(2)}) collective-permute-start(bf16[256,256]{1,0:T(8,128)(2,1)S(1)} %maximum_maximum_fusion), channel_id=1, source_target_pairs={{0,16},{1,49},{2,18},{3,51},{4,20},{5,53},{6,22},{7,55},{8,24},{9,... | collective-permute-start | bytes 393224 | tf_op jit(solution)/shard_map/ppermute | solution.py:46
  6.2 14.1 %collective-permute-start.4 = (bf16[256,256]{1,0:T(8,128)(2,1)S(1)}, bf16[256,256]{1,0:T(8,128)(2,1)S(1)}, u32[]{:S(2)}, u32[]{:S(2)}) collective-permute-start(bf16[256,256]{1,0:T(8,128)(2,1)S(1)} %maximum_maximum_fusion), channel_id=1, source_target_pairs={{0,12},{1,45},{2,14},{3,47},{4,8},{5,41},{6,10},{7,43},{8,20},{9,5... | collective-permute-start | bytes 393224 | tf_op jit(solution)/shard_map/ppermute | solution.py:46
  10.7 12.4 %collective-permute-start.5 = (bf16[256,256]{1,0:T(8,128)(2,1)S(1)}, bf16[256,256]{1,0:T(8,128)(2,1)S(1)}, u32[]{:S(2)}, u32[]{:S(2)}) collective-permute-start(bf16[256,256]{1,0:T(8,128)(2,1)S(1)} %maximum_maximum_fusion), channel_id=1, source_target_pairs={{0,28},{1,61},{2,30},{3,63},{4,24},{5,57},{6,26},{7,59},{8,36},{9,... | collective-permute-start | bytes 393224 | tf_op jit(solution)/shard_map/ppermute | solution.py:46
  14.5 8.0 %collective-permute-start.3 = (bf16[128,256]{1,0:T(8,128)(2,1)S(1)}, bf16[128,256]{1,0:T(8,128)(2,1)S(1)}, u32[]{:S(2)}, u32[]{:S(2)}) collective-permute-start(bf16[128,256]{1,0:T(8,128)(2,1)S(1)} %slice.71), channel_id=1, source_target_pairs={{0,16},{1,49},{2,18},{3,51},{4,20},{5,53},{6,22},{7,55},{8,24},{9,... | collective-permute-start | bytes 196616 | tf_op jit(solution)/shard_map/ppermute | solution.py:46
  15.3 0.8 copy-start.2
  16.1 0.7 copy-start.3
  16.7 0.7 copy-start.4
  22.6 32.1 %copy-start = (bf16[128,1024]{1,0:T(8,128)(2,1)S(1)}, bf16[128,1024]{1,0:T(8,128)(2,1)}, u32[]{:S(2)}) copy-start(bf16[128,1024]{1,0:T(8,128)(2,1)} %query.1) | copy-start | bytes 786436
  22.6 32.1 %copy-start.1 = (bf16[128,1024]{1,0:T(8,128)(2,1)S(1)}, bf16[128,1024]{1,0:T(8,128)(2,1)}, u32[]{:S(2)}) copy-start(bf16[128,1024]{1,0:T(8,128)(2,1)} %grad_out.1) | copy-start | bytes 786436
  23.1 14.3 %collective-permute-start.7 = (bf16[1024,256]{1,0:T(8,128)(2,1)S(1)}, bf16[1024,256]{1,0:T(8,128)(2,1)S(1)}, u32[]{:S(2)}, u32[]{:S(2)}) collective-permute-start(bf16[1024,256]{1,0:T(8,128)(2,1)S(1)} %constant_dynamic-update-slice_fusion.2.refs_0_), channel_id=1, source_target_pairs={{0,6},{1,7},{2,0},{3,1},{4,2},{5,3},{6,4},{7,5},{8,14},{9,15},{10,... | collective-permute-start | bytes 1572872 | tf_op jit(solution)/shard_map/ppermute | solution.py:46
  25.4 15.4 %collective-permute-start.6 = (bf16[1024,256]{1,0:T(8,128)(2,1)S(1)}, bf16[1024,256]{1,0:T(8,128)(2,1)S(1)}, u32[]{:S(2)}, u32[]{:S(2)}) collective-permute-start(bf16[1024,256]{1,0:T(8,128)(2,1)S(1)} %constant_dynamic-update-slice_fusion.2.refs_0_), channel_id=1, source_target_pairs={{0,2},{1,3},{2,4},{3,5},{4,6},{5,7},{6,0},{7,1},{8,10},{9,11},{10,... | collective-permute-start | bytes 1572872 | tf_op jit(solution)/shard_map/ppermute | solution.py:46
  25.5 15.4 %collective-permute-start.9 = (bf16[512,256]{1,0:T(8,128)(2,1)S(1)}, bf16[512,256]{1,0:T(8,128)(2,1)S(1)}, u32[]{:S(2)}, u32[]{:S(2)}) collective-permute-start(bf16[512,256]{1,0:T(8,128)(2,1)S(1)} %pad_maximum_fusion), channel_id=1, source_target_pairs={{0,56},{1,57},{2,58},{3,59},{4,60},{5,61},{6,62},{7,63},{8,0},{9,1... | collective-permute-start | bytes 786440 | tf_op jit(solution)/shard_map/ppermute | solution.py:46
  27.0 14.3 %collective-permute-start.8 = (bf16[512,256]{1,0:T(8,128)(2,1)S(1)}, bf16[512,256]{1,0:T(8,128)(2,1)S(1)}, u32[]{:S(2)}, u32[]{:S(2)}) collective-permute-start(bf16[512,256]{1,0:T(8,128)(2,1)S(1)} %pad_maximum_fusion), channel_id=1, source_target_pairs={{0,8},{1,9},{2,10},{3,11},{4,12},{5,13},{6,14},{7,15},{8,16},{9,17... | collective-permute-start | bytes 786440 | tf_op jit(solution)/shard_map/ppermute | solution.py:46
  28.2 13.2 %collective-permute-start.10 = (bf16[1024,256]{1,0:T(8,128)(2,1)S(1)}, bf16[1024,256]{1,0:T(8,128)(2,1)S(1)}, u32[]{:S(2)}, u32[]{:S(2)}) collective-permute-start(bf16[1024,256]{1,0:T(8,128)(2,1)S(1)} %constant_dynamic-update-slice_fusion.2.refs_0_), channel_id=1, source_target_pairs={{0,1},{1,0},{2,3},{3,2},{4,5},{5,4},{6,7},{7,6},{8,9},{9,8},{10,11... | collective-permute-start | bytes 1572872 | tf_op jit(solution)/shard_map/ppermute | solution.py:46
  37.4 6.1 %collective-permute-start.12 = (bf16[1024,256]{1,0:T(8,128)(2,1)S(1)}, bf16[1024,256]{1,0:T(8,128)(2,1)S(1)}, u32[]{:S(2)}, u32[]{:S(2)}) collective-permute-start(bf16[1024,256]{1,0:T(8,128)(2,1)S(1)} %collective-permute-done.7.refs_2_), channel_id=1, source_target_pairs={{0,1},{1,0},{2,3},{3,2},{4,5},{5,4},{6,7},{7,6},{8,9},{9,8},{10,11... | collective-permute-start | bytes 1572872 | tf_op jit(solution)/shard_map/ppermute | solution.py:46
  40.9 2.7 %collective-permute-start.11 = (bf16[1024,256]{1,0:T(8,128)(2,1)S(1)}, bf16[1024,256]{1,0:T(8,128)(2,1)S(1)}, u32[]{:S(2)}, u32[]{:S(2)}) collective-permute-start(bf16[1024,256]{1,0:T(8,128)(2,1)S(1)} %collective-permute-done.6.refs_1_), channel_id=1, source_target_pairs={{0,1},{1,0},{2,3},{3,2},{4,5},{5,4},{6,7},{7,6},{8,9},{9,8},{10,11... | collective-permute-start | bytes 1572872 | tf_op jit(solution)/shard_map/ppermute | solution.py:46
  40.9 2.3 %collective-permute-start.14 = (bf16[512,256]{1,0:T(8,128)(2,1)S(1)}, bf16[512,256]{1,0:T(8,128)(2,1)S(1)}, u32[]{:S(2)}, u32[]{:S(2)}) collective-permute-start(bf16[512,256]{1,0:T(8,128)(2,1)S(1)} %collective-permute-done.9.refs_4_), channel_id=1, source_target_pairs={{0,1},{1,0},{2,3},{3,2},{4,5},{5,4},{6,7},{7,6},{8,9},{9,8},{10,11... | collective-permute-start | bytes 786440 | tf_op jit(solution)/shard_map/ppermute | solution.py:46
  41.4 2.1 %collective-permute-start.13 = (bf16[512,256]{1,0:T(8,128)(2,1)S(1)}, bf16[512,256]{1,0:T(8,128)(2,1)S(1)}, u32[]{:S(2)}, u32[]{:S(2)}) collective-permute-start(bf16[512,256]{1,0:T(8,128)(2,1)S(1)} %collective-permute-done.8.refs_3_), channel_id=1, source_target_pairs={{0,1},{1,0},{2,3},{3,2},{4,5},{5,4},{6,7},{7,6},{8,9},{9,8},{10,11... | collective-permute-start | bytes 786440 | tf_op jit(solution)/shard_map/ppermute | solution.py:46
  44.5 8.4 %collective-permute-start.15 = (bf16[1024,128]{1,0:T(8,128)(2,1)S(1)}, bf16[1024,128]{1,0:T(8,128)(2,1)S(1)}, u32[]{:S(2)}, u32[]{:S(2)}) collective-permute-start(bf16[1024,128]{1,0:T(8,128)(2,1)S(1)} %get-tuple-element.47), channel_id=1, source_target_pairs={{0,64},{64,128},{128,192},{192,0},{1,65},{65,129},{129,193},{193,1... | collective-permute-start | bytes 786440 | tf_op jit(solution)/shard_map/ppermute | solution.py:442
  52.9 1.7 %collective-permute-start.16 = (bf16[1024,128]{1,0:T(8,128)(2,1)S(1)}, bf16[1024,128]{1,0:T(8,128)(2,1)S(1)}, u32[]{:S(2)}, u32[]{:S(2)}) collective-permute-start(bf16[1024,128]{1,0:T(8,128)(2,1)S(1)} %collective-permute-done.15.refs_10_), channel_id=1, source_target_pairs={{0,1},{1,0},{2,3},{3,2},{4,5},{5,4},{6,7},{7,6},{8,9},{9,8},{10,11... | collective-permute-start | bytes 786440 | tf_op jit(solution)/shard_map/ppermute | solution.py:46
  52.9 9.2 %collective-permute-start.18 = (bf16[1024,128]{1,0:T(8,128)(2,1)S(1)}, bf16[1024,128]{1,0:T(8,128)(2,1)S(1)}, u32[]{:S(2)}, u32[]{:S(2)}) collective-permute-start(bf16[1024,128]{1,0:T(8,128)(2,1)S(1)} %get-tuple-element.55), channel_id=1, source_target_pairs={{0,64},{64,128},{128,192},{192,0},{1,65},{65,129},{129,193},{193,1... | collective-permute-start | bytes 786440 | tf_op jit(solution)/shard_map/ppermute | solution.py:442
  61.8 1.6 %collective-permute-start.17 = (bf16[1024,128]{1,0:T(8,128)(2,1)S(1)}, bf16[1024,128]{1,0:T(8,128)(2,1)S(1)}, u32[]{:S(2)}, u32[]{:S(2)}) collective-permute-start(bf16[1024,128]{1,0:T(8,128)(2,1)S(1)} %get-tuple-element.50), channel_id=1, source_target_pairs={{0,1},{1,0},{2,3},{3,2},{4,5},{5,4},{6,7},{7,6},{8,9},{9,8},{10,11... | collective-permute-start | bytes 786440 | tf_op jit(solution)/shard_map/ppermute | solution.py:46
  62.2 2.1 %collective-permute-start.19 = (bf16[1024,128]{1,0:T(8,128)(2,1)S(1)}, bf16[1024,128]{1,0:T(8,128)(2,1)S(1)}, u32[]{:S(2)}, u32[]{:S(2)}) collective-permute-start(bf16[1024,128]{1,0:T(8,128)(2,1)S(1)} %collective-permute-done.18.refs_10_), channel_id=1, source_target_pairs={{0,1},{1,0},{2,3},{3,2},{4,5},{5,4},{6,7},{7,6},{8,9},{9,8},{10,11... | collective-permute-start | bytes 786440 | tf_op jit(solution)/shard_map/ppermute | solution.py:46
  63.5 9.7 %collective-permute-start.20 = (bf16[1024,128]{1,0:T(8,128)(2,1)S(1)}, bf16[1024,128]{1,0:T(8,128)(2,1)S(1)}, u32[]{:S(2)}, u32[]{:S(2)}) collective-permute-start(bf16[1024,128]{1,0:T(8,128)(2,1)S(1)} %add_convert_fusion.5), channel_id=1, source_target_pairs={{64,0},{128,64},{192,128},{0,192},{65,1},{129,65},{193,129},{1,193... | collective-permute-start | bytes 786440 | tf_op jit(solution)/shard_map/ppermute | solution.py:448
  73.3 1.5 %collective-permute-start.21 = (bf16[1024,128]{1,0:T(8,128)(2,1)S(1)}, bf16[1024,128]{1,0:T(8,128)(2,1)S(1)}, u32[]{:S(2)}, u32[]{:S(2)}) collective-permute-start(bf16[1024,128]{1,0:T(8,128)(2,1)S(1)} %get-tuple-element.63), channel_id=1, source_target_pairs={{0,1},{1,0},{2,3},{3,2},{4,5},{5,4},{6,7},{7,6},{8,9},{9,8},{10,11... | collective-permute-start | bytes 786440 | tf_op jit(solution)/shard_map/ppermute | solution.py:46
  74.9 9.6 %collective-permute-start.22 = (bf16[1024,128]{1,0:T(8,128)(2,1)S(1)}, bf16[1024,128]{1,0:T(8,128)(2,1)S(1)}, u32[]{:S(2)}, u32[]{:S(2)}) collective-permute-start(bf16[1024,128]{1,0:T(8,128)(2,1)S(1)} %add_convert_fusion.4), channel_id=1, source_target_pairs={{64,0},{128,64},{192,128},{0,192},{65,1},{129,65},{193,129},{1,193... | collective-permute-start | bytes 786440 | tf_op jit(solution)/shard_map/ppermute | solution.py:452
  86.4 2.0 %collective-permute-start.24 = (bf16[1024,256]{1,0:T(8,128)(2,1)S(1)}, bf16[1024,256]{1,0:T(8,128)(2,1)S(1)}, u32[]{:S(2)}, u32[]{:S(2)}) collective-permute-start(bf16[1024,256]{1,0:T(8,128)(2,1)S(1)} %get-tuple-element.68), channel_id=1, source_target_pairs={{0,1},{1,0},{2,3},{3,2},{4,5},{5,4},{6,7},{7,6},{8,9},{9,8},{10,11... | collective-permute-start | bytes 1572872 | tf_op jit(solution)/shard_map/ppermute | solution.py:46
  86.5 3.2 %collective-permute-start.26 = (bf16[1024,256]{1,0:T(8,128)(2,1)S(1)}, bf16[1024,256]{1,0:T(8,128)(2,1)S(1)}, u32[]{:S(2)}, u32[]{:S(2)}) collective-permute-start(bf16[1024,256]{1,0:T(8,128)(2,1)S(1)} %get-tuple-element.70), channel_id=1, source_target_pairs={{0,1},{1,0},{2,3},{3,2},{4,5},{5,4},{6,7},{7,6},{8,9},{9,8},{10,11... | collective-permute-start | bytes 1572872 | tf_op jit(solution)/shard_map/ppermute | solution.py:46
  87.0 3.9 %collective-permute-start.28 = (bf16[512,256]{1,0:T(8,128)(2,1)S(1)}, bf16[512,256]{1,0:T(8,128)(2,1)S(1)}, u32[]{:S(2)}, u32[]{:S(2)}) collective-permute-start(bf16[512,256]{1,0:T(8,128)(2,1)S(1)} %get-tuple-element.72), channel_id=1, source_target_pairs={{0,1},{1,0},{2,3},{3,2},{4,5},{5,4},{6,7},{7,6},{8,9},{9,8},{10,11... | collective-permute-start | bytes 786440 | tf_op jit(solution)/shard_map/ppermute | solution.py:46
  87.1 6.1 %collective-permute-start.23 = (bf16[1024,256]{1,0:T(8,128)(2,1)S(1)}, bf16[1024,256]{1,0:T(8,128)(2,1)S(1)}, u32[]{:S(2)}, u32[]{:S(2)}) collective-permute-start(bf16[1024,256]{1,0:T(8,128)(2,1)S(1)} %get-tuple-element.66), channel_id=1, source_target_pairs={{0,1},{1,0},{2,3},{3,2},{4,5},{5,4},{6,7},{7,6},{8,9},{9,8},{10,11... | collective-permute-start | bytes 1572872 | tf_op jit(solution)/shard_map/ppermute | solution.py:46
  88.5 14.0 %collective-permute-start.25 = (bf16[1024,256]{1,0:T(8,128)(2,1)S(1)}, bf16[1024,256]{1,0:T(8,128)(2,1)S(1)}, u32[]{:S(2)}, u32[]{:S(2)}) collective-permute-start(bf16[1024,256]{1,0:T(8,128)(2,1)S(1)} %add_convert_fusion.1), channel_id=1, source_target_pairs={{0,6},{1,7},{2,0},{3,1},{4,2},{5,3},{6,4},{7,5},{8,14},{9,15},{10,... | collective-permute-start | bytes 1572872 | tf_op jit(solution)/shard_map/ppermute | solution.py:46
  89.8 15.0 %collective-permute-start.27 = (bf16[1024,256]{1,0:T(8,128)(2,1)S(1)}, bf16[1024,256]{1,0:T(8,128)(2,1)S(1)}, u32[]{:S(2)}, u32[]{:S(2)}) collective-permute-start(bf16[1024,256]{1,0:T(8,128)(2,1)S(1)} %add_convert_fusion), channel_id=1, source_target_pairs={{0,2},{1,3},{2,4},{3,5},{4,6},{5,7},{6,0},{7,1},{8,10},{9,11},{10,... | collective-permute-start | bytes 1572872 | tf_op jit(solution)/shard_map/ppermute | solution.py:46
  90.9 1.5 %collective-permute-start.30 = (bf16[512,256]{1,0:T(8,128)(2,1)S(1)}, bf16[512,256]{1,0:T(8,128)(2,1)S(1)}, u32[]{:S(2)}, u32[]{:S(2)}) collective-permute-start(bf16[512,256]{1,0:T(8,128)(2,1)S(1)} %get-tuple-element.74), channel_id=1, source_target_pairs={{0,1},{1,0},{2,3},{3,2},{4,5},{5,4},{6,7},{7,6},{8,9},{9,8},{10,11... | collective-permute-start | bytes 786440 | tf_op jit(solution)/shard_map/ppermute | solution.py:46
  90.9 14.1 %collective-permute-start.29 = (bf16[512,256]{1,0:T(8,128)(2,1)S(1)}, bf16[512,256]{1,0:T(8,128)(2,1)S(1)}, u32[]{:S(2)}, u32[]{:S(2)}) collective-permute-start(bf16[512,256]{1,0:T(8,128)(2,1)S(1)} %add_convert_fusion.3), channel_id=1, source_target_pairs={{0,56},{1,57},{2,58},{3,59},{4,60},{5,61},{6,62},{7,63},{8,0},{9,1... | collective-permute-start | bytes 786440 | tf_op jit(solution)/shard_map/ppermute | solution.py:46
  92.5 12.6 %collective-permute-start.31 = (bf16[512,256]{1,0:T(8,128)(2,1)S(1)}, bf16[512,256]{1,0:T(8,128)(2,1)S(1)}, u32[]{:S(2)}, u32[]{:S(2)}) collective-permute-start(bf16[512,256]{1,0:T(8,128)(2,1)S(1)} %add_convert_fusion.2), channel_id=1, source_target_pairs={{0,8},{1,9},{2,10},{3,11},{4,12},{5,13},{6,14},{7,15},{8,16},{9,17... | collective-permute-start | bytes 786440 | tf_op jit(solution)/shard_map/ppermute | solution.py:46
  105.2 8.5 %collective-permute-start.32 = (bf16[384,256]{1,0:T(8,128)(2,1)S(1)}, bf16[384,256]{1,0:T(8,128)(2,1)S(1)}, u32[]{:S(2)}, u32[]{:S(2)}) collective-permute-start(bf16[384,256]{1,0:T(8,128)(2,1)S(1)} %pad_maximum_fusion.1), channel_id=1, source_target_pairs={{0,48},{1,17},{2,50},{3,19},{4,52},{5,21},{6,54},{7,23},{8,56},{9,... | collective-permute-start | bytes 589832 | tf_op jit(solution)/shard_map/ppermute | solution.py:46
  106.4 10.9 %collective-permute-start.35 = (bf16[256,256]{1,0:T(8,128)(2,1)S(1)}, bf16[256,256]{1,0:T(8,128)(2,1)S(1)}, u32[]{:S(2)}, u32[]{:S(2)}) collective-permute-start(bf16[256,256]{1,0:T(8,128)(2,1)S(1)} %slice.79), channel_id=1, source_target_pairs={{0,44},{1,13},{2,46},{3,15},{4,40},{5,9},{6,42},{7,11},{8,52},{9,2... | collective-permute-start | bytes 393224 | tf_op jit(solution)/shard_map/ppermute | solution.py:46
  108.1 10.4 %collective-permute-start.34 = (bf16[256,256]{1,0:T(8,128)(2,1)S(1)}, bf16[256,256]{1,0:T(8,128)(2,1)S(1)}, u32[]{:S(2)}, u32[]{:S(2)}) collective-permute-start(bf16[256,256]{1,0:T(8,128)(2,1)S(1)} %slice.77), channel_id=1, source_target_pairs={{0,60},{1,29},{2,62},{3,31},{4,56},{5,25},{6,58},{7,27},{8,4},{9,3... | collective-permute-start | bytes 393224 | tf_op jit(solution)/shard_map/ppermute | solution.py:46
  113.8 6.1 %collective-permute-start.33 = (bf16[128,256]{1,0:T(8,128)(2,1)S(1)}, bf16[128,256]{1,0:T(8,128)(2,1)S(1)}, u32[]{:S(2)}, u32[]{:S(2)}) collective-permute-start(bf16[128,256]{1,0:T(8,128)(2,1)S(1)} %slice.75), channel_id=1, source_target_pairs={{0,48},{1,17},{2,50},{3,19},{4,52},{5,21},{6,54},{7,23},{8,56},{9,... | collective-permute-start | bytes 196616 | tf_op jit(solution)/shard_map/ppermute | solution.py:46
  118.6 1.7 %collective-permute-start.36 = (bf16[128,256]{1,0:T(8,128)(2,1)S(1)}, bf16[128,256]{1,0:T(8,128)(2,1)S(1)}, u32[]{:S(2)}, u32[]{:S(2)}) collective-permute-start(bf16[128,256]{1,0:T(8,128)(2,1)S(1)} %add_convert_fusion.6), channel_id=1, source_target_pairs={{0,1},{1,0},{2,3},{3,2},{4,5},{5,4},{6,7},{7,6},{8,9},{9,8},{10,11... | collective-permute-start | bytes 196616 | tf_op jit(solution)/shard_map/ppermute | solution.py:46
where the time goes:
time: 122 us; the launch traced here: 121 us
  waiting for transfers between devices  58.6 us (48%)
  starting transfers between devices  36.3 us (30%)
  Pallas kernels  19.7 us (16%)
  local copies, waits for them, and re-layouts  4.37 us (4%)
    ppermute x33, waiting for transfers between devices, send(): return lax.ppermute(value, 'local', moves(by_core))  39.1 us
    ppermute x33, starting transfers between devices, send(): return lax.ppermute(value, 'local', moves(by_core))  33.2 us
    ppermute x1, waiting for transfers between devices, per_device(): tail_keys = lax.ppermute(tail_keys, 'node', backward)  9.54 us
    ppermute x2, waiting for transfers between devices, per_device(): lax.ppermute(tail, 'node', onward)  7.87 us
    pallas_call x1, Pallas kernels, on_keys(): pl.pallas_call(key_kernel, out_shape=(jax.ShapeDtypeStruct((2, WINDOW, CO...  7.19 us
    pallas_call x1, Pallas kernels, on_values(): pl.pallas_call(value_kernel, out_shape=(shape(2 * STRETCH, HEADS * HEAD_D...  6.83 us
    unnamed x15, local copies, waits for them, and re-layouts  3.68 us
    pallas_call x1, Pallas kernels, plan(): pl.pallas_call(plan_kernel, out_shape=tuple((jax.ShapeDtypeStruct((n,), j...  2.82 us
  transfers between devices with their start and end apart: 37, of which 20 were waited for; matrix products, arithmetic and copies ran while one was open for 2% of the time, Pallas kernels for 14%

commit v1 on v0

--- a/solution.py
+++ b/solution.py
@@ -159,25 +159,24 @@
     )(stretch_order, reach, jnp.asarray(TABLE))
 
 
-def pick_kernel(places, *refs):
-    pieces, keys, values, held = refs[: len(PIECES)], *refs[len(PIECES) :]
-    lay(pieces, held)
+def pick_kernel(part, places, *refs):
+    pieces, (out, held) = refs[: len(PIECES)], refs[len(PIECES) :]
+    lay(pieces, held, pl.ds(part * HEAD_DIM, HEAD_DIM))
 
     def one(i, carry):
-        rows = held[at(places[i])]
-        keys[at(i)], values[at(i)] = rows[:, :HEAD_DIM], rows[:, HEAD_DIM:]
-        return carry
-
-    lax.fori_loop(0, TAIL, one, 0)
-
-
-def pick(places, pieces):
+        out[at(i)] = held[at(places[i])]
+        return carry
+
+    lax.fori_loop(0, TAIL, one, 0, unroll=4)
+
+
+def pick(part, places, pieces):
     return pl.pallas_call(
-        pick_kernel,
-        out_shape=(shape(TAIL * STRETCH),) * 2,
+        functools.partial(pick_kernel, part),
+        out_shape=shape(TAIL * STRETCH),
         in_specs=[SMEM] + [VMEM] * len(pieces),
-        out_specs=(VMEM,) * 2,
-        scratch_shapes=[pltpu.VMEM((SLOTS * STRETCH, 2 * HEAD_DIM), jnp.bfloat16)],
+        out_specs=VMEM,
+        scratch_shapes=[pltpu.VMEM((SLOTS * STRETCH, HEAD_DIM), jnp.bfloat16)],
         compiler_params=small(PICK_KIB),
         name="pick_tail",
     )(places, *pieces)
@@ -302,8 +301,7 @@
         dq = 0.0
         for j in range(CHUNKS):
             rows = pl.ds(j * CHUNK, CHUNK)
-            prob = prob_in[c, rows].astype(jnp.float32)
-            dscore = (prob * (dprob[c, rows] - delta)).astype(jnp.bfloat16)
+            dscore = prob_in[c, rows] * (dprob[c, rows] - delta).astype(jnp.bfloat16)
             terms[c, rows] = dot(dscore, q, (1, 0)) * scale
             dq = dq + dot(keys_in[c, rows], dscore, (0, 0))
         dq = (jnp.transpose(dq) * scale).astype(jnp.bfloat16)
@@ -439,7 +437,7 @@
     own, other = [jnp.concatenate(rows, axis=1) for rows in ((key, value), (swap(key), swap(value)))]
     pieces = gather_block(own, other, unit, send, join, settle)
     places, tail_places, facts = tables
-    tails = [lax.ppermute(tail, "node", onward) for tail in pick(tail_places, pieces)]
+    tails = [lax.ppermute(pick(part, tail_places, pieces), "node", onward) for part in (0, 1)]
     keys, values = [pieces + [tail, swap(tail)] for tail in tails]
 
     *carried, block_values, own_tail, other_tail = on_keys(places, facts, query, grad_out, keys)

time: 122 us -> 123 us (level)
  transfers between devices with their start and end apart: 37 -> 37, of which waited for: 20 -> 20; matrix products, arithmetic and copies ran while one was open for 2% -> 2% of each run, Pallas kernels for 14% -> 15%
where the time goes in v1:
time: 123 us; the launch traced here: 122 us
  waiting for transfers between devices  59 us (48%)
  starting transfers between devices  36.1 us (29%)
  Pallas kernels  20.6 us (17%)
  local copies, waits for them, and re-layouts  4.37 us (4%)
    ppermute x33, waiting for transfers between devices, send(): return lax.ppermute(value, 'local', moves(by_core))  39.1 us
    ppermute x33, starting transfers between devices, send(): return lax.ppermute(value, 'local', moves(by_core))  33.2 us
    ppermute x1, waiting for transfers between devices, per_device(): tail_keys = lax.ppermute(tail_keys, 'node', backward)  9.54 us
    ppermute x2, waiting for transfers between devices, per_device(): lax.ppermute(pick(part, tail_places, pieces), 'node', onward)  7.87 us
    pallas_call x1, Pallas kernels, on_keys(): pl.pallas_call(key_kernel, out_shape=(jax.ShapeDtypeStruct((2, WINDOW, CO...  7.2 us
    pallas_call x1, Pallas kernels, on_values(): pl.pallas_call(value_kernel, out_shape=(shape(2 * STRETCH, HEADS * HEAD_D...  6.79 us
    unnamed x15, local copies, waits for them, and re-layouts  3.68 us
    pallas_call x1, Pallas kernels, plan(): pl.pallas_call(plan_kernel, out_shape=tuple((jax.ShapeDtypeStruct((n,), j...  2.82 us
  transfers between devices with their start and end apart: 37, of which 20 were waited for; matrix products, arithmetic and copies ran while one was open for 2% of the time, Pallas kernels for 15%

profile of v1, /device:TPU:6, one launch (start us, length us, event | category | flops | bytes accessed | tf_op | source)
XLA Modules:
  0.0 122.0 jit_solution(11243814448618966325)
XLA Ops:
  0.6 0.1 collective-permute-start
  0.7 0.5 collective-permute-start.1
  1.2 0.8 constant_dynamic-update-slice_fusion.7
  2.0 0.8 constant_dynamic-update-slice_fusion.6
  2.8 3.3 %collective-permute-start.2 = (bf16[256,256]{1,0:T(8,128)(2,1)S(1)}, bf16[256,256]{1,0:T(8,128)(2,1)S(1)}, u32[]{:S(2)}, u32[]{:S(2)}) collective-permute-start(bf16[256,256]{1,0:T(8,128)(2,1)S(1)} %maximum_maximum_fusion), channel_id=1, source_target_pairs={{0,16},{1,49},{2,18},{3,51},{4,20},{5,53},{6,22},{7,55},{8,24},{9,... | collective-permute-start | bytes 393224 | tf_op jit(solution)/shard_map/ppermute | solution.py:46
  6.2 4.5 %collective-permute-start.4 = (bf16[256,256]{1,0:T(8,128)(2,1)S(1)}, bf16[256,256]{1,0:T(8,128)(2,1)S(1)}, u32[]{:S(2)}, u32[]{:S(2)}) collective-permute-start(bf16[256,256]{1,0:T(8,128)(2,1)S(1)} %maximum_maximum_fusion), channel_id=1, source_target_pairs={{0,12},{1,45},{2,14},{3,47},{4,8},{5,41},{6,10},{7,43},{8,20},{9,5... | collective-permute-start | bytes 393224 | tf_op jit(solution)/shard_map/ppermute | solution.py:46
  10.7 3.8 %collective-permute-start.5 = (bf16[256,256]{1,0:T(8,128)(2,1)S(1)}, bf16[256,256]{1,0:T(8,128)(2,1)S(1)}, u32[]{:S(2)}, u32[]{:S(2)}) collective-permute-start(bf16[256,256]{1,0:T(8,128)(2,1)S(1)} %maximum_maximum_fusion), channel_id=1, source_target_pairs={{0,28},{1,61},{2,30},{3,63},{4,24},{5,57},{6,26},{7,59},{8,36},{9,... | collective-permute-start | bytes 393224 | tf_op jit(solution)/shard_map/ppermute | solution.py:46
  14.5 0.8 collective-permute-start.3
  15.3 0.8 copy-done.2
  16.1 0.7 copy-done.3
  16.7 0.7 copy-done.4
  17.4 2.8 %plan.1 = (s32[66]{0:T(128)S(1)}, s32[16]{0:T(128)S(1)}, s32[5]{0:T(128)S(1)}) custom-call(s32[4,128]{1,0:T(4,128)S(1)} %copy-done.3, s32[4]{0:T(128)S(1)} %copy-done.4, s32[64,128]{1,0:T(8,128)S(1)} %copy-done.2), custom_call_target="tpu_custom_call" | custom-call | tf_op jit(solution)/shard_map/plan/pallas_call | solution.py:151
  20.3 2.3 %collective-permute-done.3 = bf16[128,256]{1,0:T(8,128)(2,1)S(1)} collective-permute-done((bf16[128,256]{1,0:T(8,128)(2,1)S(1)}, bf16[128,256]{1,0:T(8,128)(2,1)S(1)}, u32[]{:S(2)}, u32[]{:S(2)}) %collective-permute-start.3) | collective-permute-done | bytes 65568 | tf_op jit(solution)/shard_map/ppermute | solution.py:46
  22.6 0.5 collective-permute-done.5
  23.1 2.3 %collective-permute-start.7 = (bf16[1024,256]{1,0:T(8,128)(2,1)S(1)}, bf16[1024,256]{1,0:T(8,128)(2,1)S(1)}, u32[]{:S(2)}, u32[]{:S(2)}) collective-permute-start(bf16[1024,256]{1,0:T(8,128)(2,1)S(1)} %constant_dynamic-update-slice_fusion.2.refs_0_), channel_id=1, source_target_pairs={{0,6},{1,7},{2,0},{3,1},{4,2},{5,3},{6,4},{7,5},{8,14},{9,15},{10,... | collective-permute-start | bytes 1572872 | tf_op jit(solution)/shard_map/ppermute | solution.py:46
  25.4 1.6 %collective-permute-start.9 = (bf16[512,256]{1,0:T(8,128)(2,1)S(1)}, bf16[512,256]{1,0:T(8,128)(2,1)S(1)}, u32[]{:S(2)}, u32[]{:S(2)}) collective-permute-start(bf16[512,256]{1,0:T(8,128)(2,1)S(1)} %pad_maximum_fusion), channel_id=1, source_target_pairs={{0,56},{1,57},{2,58},{3,59},{4,60},{5,61},{6,62},{7,63},{8,0},{9,1... | collective-permute-start | bytes 786440 | tf_op jit(solution)/shard_map/ppermute | solution.py:46
  27.0 1.2 collective-permute-start.8
  28.2 9.2 %collective-permute-done.7.refs_2_ = bf16[1024,256]{1,0:T(8,128)(2,1)S(1)} collective-permute-done((bf16[1024,256]{1,0:T(8,128)(2,1)S(1)}, bf16[1024,256]{1,0:T(8,128)(2,1)S(1)}, u32[]{:S(2)}, u32[]{:S(2)}) %collective-permute-start.7) | collective-permute-done | bytes 524320 | tf_op jit(solution)/shard_map/ppermute | solution.py:46
  37.4 3.4 %collective-permute-done.6.refs_1_ = bf16[1024,256]{1,0:T(8,128)(2,1)S(1)} collective-permute-done((bf16[1024,256]{1,0:T(8,128)(2,1)S(1)}, bf16[1024,256]{1,0:T(8,128)(2,1)S(1)}, u32[]{:S(2)}, u32[]{:S(2)}) %collective-permute-start.6) | collective-permute-done | bytes 524320 | tf_op jit(solution)/shard_map/ppermute | solution.py:46
  40.8 0.5 collective-permute-start.14
  41.3 0.1 collective-permute-start.13
  41.4 1.7 %collective-permute-done.14.refs_9_ = bf16[512,256]{1,0:T(8,128)(2,1)S(1)} collective-permute-done((bf16[512,256]{1,0:T(8,128)(2,1)S(1)}, bf16[512,256]{1,0:T(8,128)(2,1)S(1)}, u32[]{:S(2)}, u32[]{:S(2)}) %collective-permute-start.14) | collective-permute-done | bytes 262176 | tf_op jit(solution)/shard_map/ppermute | solution.py:46
  43.1 0.4 collective-permute-done.13.refs_8_
  43.5 1.0 pick_tail.2
  44.5 0.6 collective-permute-start.15
  45.0 7.9 %collective-permute-done.15.refs_10_ = bf16[1024,128]{1,0:T(8,128)(2,1)S(1)} collective-permute-done((bf16[1024,128]{1,0:T(8,128)(2,1)S(1)}, bf16[1024,128]{1,0:T(8,128)(2,1)S(1)}, u32[]{:S(2)}, u32[]{:S(2)}) %collective-permute-start.15) | collective-permute-done | bytes 262176 | tf_op jit(solution)/shard_map/ppermute | solution.py:440
  52.9 1.0 pick_tail.3
  53.9 1.8 %collective-permute-start.18 = (bf16[1024,128]{1,0:T(8,128)(2,1)S(1)}, bf16[1024,128]{1,0:T(8,128)(2,1)S(1)}, u32[]{:S(2)}, u32[]{:S(2)}) collective-permute-start(bf16[1024,128]{1,0:T(8,128)(2,1)S(1)} %pick_tail.3), channel_id=1, source_target_pairs={{0,64},{64,128},{128,192},{192,0},{1,65},{65,129},{129,193},{193,1... | collective-permute-start | bytes 786440 | tf_op jit(solution)/shard_map/ppermute | solution.py:440
  55.7 7.2 %on_keys.1 = (bf16[2,2112,512]{2,1,0:T(8,128)(2,1)S(1)}, bf16[2,2112,128]{2,1,0:T(8,128)(2,1)S(1)}, bf16[2,512,128]{2,1,0:T(8,128)(2,1)S(1)}, bf16[2,512,128]{2,...) custom-call(s32[66]{0:T(128)S(1)} %get-tuple-element.41.places, ...), custom_call_target="tpu_custom_call" | custom-call | tf_op jit(solution)/shard_map/on_keys/pallas_call | solution.py:331
  62.9 0.3 collective-permute-start.17
  63.2 0.3 collective-permute-start.19
  63.5 1.0 collective-permute-done.17
  64.6 0.4 collective-permute-start.20
  65.0 6.8 %on_values.1 = (bf16[128,1024]{1,0:T(8,128)(2,1)}, bf16[10304,128]{1,0:T(8,128)(2,1)S(1)}, bf16[1024,128]{1,0:T(8,128)(2,1)S(1)}, bf16[1024,128]{1,0:T(8,128)(2,1)S(1)}) custom-call(s32[66]{0:T(128)S(1)} %get-tuple-element.41.places, s32[5]{0:T(128)S(1)} %get-tuple-element.42.facts, bf16[2,2112,512]{2,1,0:T(8,128)(2,1)S(1)} %get-tuple-element.48.prob_in, ...), custom_call_target="tpu_custom_call" | custom-call | flops 3321888768 | bytes 12582912 | tf_op jit(solution)/shard_map/on_values/pallas_call | solution.py:353
  71.8 2.5 %collective-permute-done.20.tail_values = bf16[1024,128]{1,0:T(8,128)(2,1)S(1)} collective-permute-done((bf16[1024,128]{1,0:T(8,128)(2,1)S(1)}, bf16[1024,128]{1,0:T(8,128)(2,1)S(1)}, u32[]{:S(2)}, u32[]{:S(2)}) %collective-permute-start.20) | collective-permute-done | bytes 262176 | tf_op jit(solution)/shard_map/ppermute | solution.py:446
  74.3 1.5 %collective-permute-done.21 = bf16[1024,128]{1,0:T(8,128)(2,1)S(1)} collective-permute-done((bf16[1024,128]{1,0:T(8,128)(2,1)S(1)}, bf16[1024,128]{1,0:T(8,128)(2,1)S(1)}, u32[]{:S(2)}, u32[]{:S(2)}) %collective-permute-start.21) | collective-permute-done | bytes 262176 | tf_op jit(solution)/shard_map/ppermute | solution.py:46
  76.0 9.5 %collective-permute-done.22.tail_keys = bf16[1024,128]{1,0:T(8,128)(2,1)S(1)} collective-permute-done((bf16[1024,128]{1,0:T(8,128)(2,1)S(1)}, bf16[1024,128]{1,0:T(8,128)(2,1)S(1)}, u32[]{:S(2)}, u32[]{:S(2)}) %collective-permute-start.22) | collective-permute-done | bytes 262176 | tf_op jit(solution)/shard_map/ppermute | solution.py:450
  85.5 1.8 %merge_tail.1 = (bf16[1024,256]{1,0:T(8,128)(2,1)S(1)}, bf16[1024,256]{1,0:T(8,128)(2,1)S(1)}, bf16[1024,256]{1,0:T(8,128)(2,1)S(1)}, bf16[512,256]{1,0:T(8,128)...) custom-call(s32[16]{0:T(128)S(1)} %get-tuple-element.44.places, ...), custom_call_target="tpu_custom_call" | custom-call | tf_op jit(solution)/shard_map/merge_tail/pallas_call | solution.py:386
  87.4 0.1 collective-permute-start.24
  87.5 0.5 collective-permute-start.26
  88.0 0.3 collective-permute-start.28
  88.3 0.2 collective-permute-start.23
  88.5 0.9 collective-permute-done.24
  89.4 0.1 add_convert_fusion.1
  89.5 1.1 collective-permute-start.25
  90.6 0.1 add_convert_fusion
  90.8 1.1 collective-permute-start.27
  92.0 1.4 %collective-permute-done.30 = bf16[512,256]{1,0:T(8,128)(2,1)S(1)} collective-permute-done((bf16[512,256]{1,0:T(8,128)(2,1)S(1)}, bf16[512,256]{1,0:T(8,128)(2,1)S(1)}, u32[]{:S(2)}, u32[]{:S(2)}) %collective-permute-start.30) | collective-permute-done | bytes 262176 | tf_op jit(solution)/shard_map/ppermute | solution.py:46
  93.5 0.7 collective-permute-start.31
  94.2 9.4 %collective-permute-done.25 = bf16[1024,256]{1,0:T(8,128)(2,1)S(1)} collective-permute-done((bf16[1024,256]{1,0:T(8,128)(2,1)S(1)}, bf16[1024,256]{1,0:T(8,128)(2,1)S(1)}, u32[]{:S(2)}, u32[]{:S(2)}) %collective-permute-start.25) | collective-permute-done | bytes 524320 | tf_op jit(solution)/shard_map/ppermute | solution.py:46
  103.6 2.2 %collective-permute-done.27 = bf16[1024,256]{1,0:T(8,128)(2,1)S(1)} collective-permute-done((bf16[1024,256]{1,0:T(8,128)(2,1)S(1)}, bf16[1024,256]{1,0:T(8,128)(2,1)S(1)}, u32[]{:S(2)}, u32[]{:S(2)}) %collective-permute-start.27) | collective-permute-done | bytes 524320 | tf_op jit(solution)/shard_map/ppermute | solution.py:46
  105.8 0.3 fusion.8
  106.1 0.1 fusion.6
  106.2 1.2 collective-permute-start.32
  107.5 1.7 %collective-permute-start.35 = (bf16[256,256]{1,0:T(8,128)(2,1)S(1)}, bf16[256,256]{1,0:T(8,128)(2,1)S(1)}, u32[]{:S(2)}, u32[]{:S(2)}) collective-permute-start(bf16[256,256]{1,0:T(8,128)(2,1)S(1)} %slice.79), channel_id=1, source_target_pairs={{0,44},{1,13},{2,46},{3,15},{4,40},{5,9},{6,42},{7,11},{8,52},{9,2... | collective-permute-start | bytes 393224 | tf_op jit(solution)/shard_map/ppermute | solution.py:46
  109.2 3.2 %collective-permute-start.34 = (bf16[256,256]{1,0:T(8,128)(2,1)S(1)}, bf16[256,256]{1,0:T(8,128)(2,1)S(1)}, u32[]{:S(2)}, u32[]{:S(2)}) collective-permute-start(bf16[256,256]{1,0:T(8,128)(2,1)S(1)} %slice.77), channel_id=1, source_target_pairs={{0,60},{1,29},{2,62},{3,31},{4,56},{5,25},{6,58},{7,27},{8,4},{9,3... | collective-permute-start | bytes 393224 | tf_op jit(solution)/shard_map/ppermute | solution.py:46
  112.4 2.4 %collective-permute-done.32 = bf16[384,256]{1,0:T(8,128)(2,1)S(1)} collective-permute-done((bf16[384,256]{1,0:T(8,128)(2,1)S(1)}, bf16[384,256]{1,0:T(8,128)(2,1)S(1)}, u32[]{:S(2)}, u32[]{:S(2)}) %collective-permute-start.32) | collective-permute-done | bytes 196640 | tf_op jit(solution)/shard_map/ppermute | solution.py:46
  114.8 3.0 %collective-permute-start.33 = (bf16[128,256]{1,0:T(8,128)(2,1)S(1)}, bf16[128,256]{1,0:T(8,128)(2,1)S(1)}, u32[]{:S(2)}, u32[]{:S(2)}) collective-permute-start(bf16[128,256]{1,0:T(8,128)(2,1)S(1)} %slice.75), channel_id=1, source_target_pairs={{0,48},{1,17},{2,50},{3,19},{4,52},{5,21},{6,54},{7,23},{8,56},{9,... | collective-permute-start | bytes 196616 | tf_op jit(solution)/shard_map/ppermute | solution.py:46
  117.8 0.5 collective-permute-done.35
  118.3 1.3 %collective-permute-done.34 = bf16[256,256]{1,0:T(8,128)(2,1)S(1)} collective-permute-done((bf16[256,256]{1,0:T(8,128)(2,1)S(1)}, bf16[256,256]{1,0:T(8,128)(2,1)S(1)}, u32[]{:S(2)}, u32[]{:S(2)}) %collective-permute-start.34) | collective-permute-done | bytes 131104 | tf_op jit(solution)/shard_map/ppermute | solution.py:46
  119.7 0.8 collective-permute-start.36
  120.4 0.4 collective-permute-done.33
  120.9 0.5 collective-permute-done.36
  121.4 0.6 fusion.9
  (51 shorter events, 0.7 us)
Async XLA Ops:
  0.6 2.2 %collective-permute-start = (bf16[128,128]{1,0:T(8,128)(2,1)}, bf16[128,128]{1,0:T(8,128)(2,1)S(1)}, u32[]{:S(2)}, u32[]{:S(2)}) collective-permute-start(bf16[128,128]{1,0:T(8,128)(2,1)} %param.8), channel_id=1, source_target_pairs={{0,1},{1,0},{2,3},{3,2},{4,5},{5,4},{6,7},{7,6},{8,9},{9,8},{10,11... | collective-permute-start | bytes 98312 | tf_op jit(solution)/shard_map/ppermute | solution.py:46
  0.7 2.1 %collective-permute-start.1 = (bf16[128,128]{1,0:T(8,128)(2,1)}, bf16[128,128]{1,0:T(8,128)(2,1)S(1)}, u32[]{:S(2)}, u32[]{:S(2)}) collective-permute-start(bf16[128,128]{1,0:T(8,128)(2,1)} %param.9), channel_id=1, source_target_pairs={{0,1},{1,0},{2,3},{3,2},{4,5},{5,4},{6,7},{7,6},{8,9},{9,8},{10,11... | collective-permute-start | bytes 98312 | tf_op jit(solution)/shard_map/ppermute | solution.py:46
  2.8 11.7 %collective-permute-start.2 = (bf16[256,256]{1,0:T(8,128)(2,1)S(1)}, bf16[256,256]{1,0:T(8,128)(2,1)S(1)}, u32[]{:S(2)}, u32[]{:S(2)}) collective-permute-start(bf16[256,256]{1,0:T(8,128)(2,1)S(1)} %maximum_maximum_fusion), channel_id=1, source_target_pairs={{0,16},{1,49},{2,18},{3,51},{4,20},{5,53},{6,22},{7,55},{8,24},{9,... | collective-permute-start | bytes 393224 | tf_op jit(solution)/shard_map/ppermute | solution.py:46
  6.2 14.1 %collective-permute-start.4 = (bf16[256,256]{1,0:T(8,128)(2,1)S(1)}, bf16[256,256]{1,0:T(8,128)(2,1)S(1)}, u32[]{:S(2)}, u32[]{:S(2)}) collective-permute-start(bf16[256,256]{1,0:T(8,128)(2,1)S(1)} %maximum_maximum_fusion), channel_id=1, source_target_pairs={{0,12},{1,45},{2,14},{3,47},{4,8},{5,41},{6,10},{7,43},{8,20},{9,5... | collective-permute-start | bytes 393224 | tf_op jit(solution)/shard_map/ppermute | solution.py:46
  10.7 12.4 %collective-permute-start.5 = (bf16[256,256]{1,0:T(8,128)(2,1)S(1)}, bf16[256,256]{1,0:T(8,128)(2,1)S(1)}, u32[]{:S(2)}, u32[]{:S(2)}) collective-permute-start(bf16[256,256]{1,0:T(8,128)(2,1)S(1)} %maximum_maximum_fusion), channel_id=1, source_target_pairs={{0,28},{1,61},{2,30},{3,63},{4,24},{5,57},{6,26},{7,59},{8,36},{9,... | collective-permute-start | bytes 393224 | tf_op jit(solution)/shard_map/ppermute | solution.py:46
  14.5 8.0 %collective-permute-start.3 = (bf16[128,256]{1,0:T(8,128)(2,1)S(1)}, bf16[128,256]{1,0:T(8,128)(2,1)S(1)}, u32[]{:S(2)}, u32[]{:S(2)}) collective-permute-start(bf16[128,256]{1,0:T(8,128)(2,1)S(1)} %slice.71), channel_id=1, source_target_pairs={{0,16},{1,49},{2,18},{3,51},{4,20},{5,53},{6,22},{7,55},{8,24},{9,... | collective-permute-start | bytes 196616 | tf_op jit(solution)/shard_map/ppermute | solution.py:46
  15.3 0.8 copy-start.2
  16.1 0.7 copy-start.3
  16.7 0.7 copy-start.4
  23.1 14.3 %collective-permute-start.7 = (bf16[1024,256]{1,0:T(8,128)(2,1)S(1)}, bf16[1024,256]{1,0:T(8,128)(2,1)S(1)}, u32[]{:S(2)}, u32[]{:S(2)}) collective-permute-start(bf16[1024,256]{1,0:T(8,128)(2,1)S(1)} %constant_dynamic-update-slice_fusion.2.refs_0_), channel_id=1, source_target_pairs={{0,6},{1,7},{2,0},{3,1},{4,2},{5,3},{6,4},{7,5},{8,14},{9,15},{10,... | collective-permute-start | bytes 1572872 | tf_op jit(solution)/shard_map/ppermute | solution.py:46
  25.4 15.4 %collective-permute-start.6 = (bf16[1024,256]{1,0:T(8,128)(2,1)S(1)}, bf16[1024,256]{1,0:T(8,128)(2,1)S(1)}, u32[]{:S(2)}, u32[]{:S(2)}) collective-permute-start(bf16[1024,256]{1,0:T(8,128)(2,1)S(1)} %constant_dynamic-update-slice_fusion.2.refs_0_), channel_id=1, source_target_pairs={{0,2},{1,3},{2,4},{3,5},{4,6},{5,7},{6,0},{7,1},{8,10},{9,11},{10,... | collective-permute-start | bytes 1572872 | tf_op jit(solution)/shard_map/ppermute | solution.py:46
  25.4 15.4 %collective-permute-start.9 = (bf16[512,256]{1,0:T(8,128)(2,1)S(1)}, bf16[512,256]{1,0:T(8,128)(2,1)S(1)}, u32[]{:S(2)}, u32[]{:S(2)}) collective-permute-start(bf16[512,256]{1,0:T(8,128)(2,1)S(1)} %pad_maximum_fusion), channel_id=1, source_target_pairs={{0,56},{1,57},{2,58},{3,59},{4,60},{5,61},{6,62},{7,63},{8,0},{9,1... | collective-permute-start | bytes 786440 | tf_op jit(solution)/shard_map/ppermute | solution.py:46
  27.0 14.3 %collective-permute-start.8 = (bf16[512,256]{1,0:T(8,128)(2,1)S(1)}, bf16[512,256]{1,0:T(8,128)(2,1)S(1)}, u32[]{:S(2)}, u32[]{:S(2)}) collective-permute-start(bf16[512,256]{1,0:T(8,128)(2,1)S(1)} %pad_maximum_fusion), channel_id=1, source_target_pairs={{0,8},{1,9},{2,10},{3,11},{4,12},{5,13},{6,14},{7,15},{8,16},{9,17... | collective-permute-start | bytes 786440 | tf_op jit(solution)/shard_map/ppermute | solution.py:46
  28.2 13.2 %collective-permute-start.10 = (bf16[1024,256]{1,0:T(8,128)(2,1)S(1)}, bf16[1024,256]{1,0:T(8,128)(2,1)S(1)}, u32[]{:S(2)}, u32[]{:S(2)}) collective-permute-start(bf16[1024,256]{1,0:T(8,128)(2,1)S(1)} %constant_dynamic-update-slice_fusion.2.refs_0_), channel_id=1, source_target_pairs={{0,1},{1,0},{2,3},{3,2},{4,5},{5,4},{6,7},{7,6},{8,9},{9,8},{10,11... | collective-permute-start | bytes 1572872 | tf_op jit(solution)/shard_map/ppermute | solution.py:46
  37.4 6.1 %collective-permute-start.12 = (bf16[1024,256]{1,0:T(8,128)(2,1)S(1)}, bf16[1024,256]{1,0:T(8,128)(2,1)S(1)}, u32[]{:S(2)}, u32[]{:S(2)}) collective-permute-start(bf16[1024,256]{1,0:T(8,128)(2,1)S(1)} %collective-permute-done.7.refs_2_), channel_id=1, source_target_pairs={{0,1},{1,0},{2,3},{3,2},{4,5},{5,4},{6,7},{7,6},{8,9},{9,8},{10,11... | collective-permute-start | bytes 1572872 | tf_op jit(solution)/shard_map/ppermute | solution.py:46
  40.8 2.7 %collective-permute-start.11 = (bf16[1024,256]{1,0:T(8,128)(2,1)S(1)}, bf16[1024,256]{1,0:T(8,128)(2,1)S(1)}, u32[]{:S(2)}, u32[]{:S(2)}) collective-permute-start(bf16[1024,256]{1,0:T(8,128)(2,1)S(1)} %collective-permute-done.6.refs_1_), channel_id=1, source_target_pairs={{0,1},{1,0},{2,3},{3,2},{4,5},{5,4},{6,7},{7,6},{8,9},{9,8},{10,11... | collective-permute-start | bytes 1572872 | tf_op jit(solution)/shard_map/ppermute | solution.py:46
  40.8 2.3 %collective-permute-start.14 = (bf16[512,256]{1,0:T(8,128)(2,1)S(1)}, bf16[512,256]{1,0:T(8,128)(2,1)S(1)}, u32[]{:S(2)}, u32[]{:S(2)}) collective-permute-start(bf16[512,256]{1,0:T(8,128)(2,1)S(1)} %collective-permute-done.9.refs_4_), channel_id=1, source_target_pairs={{0,1},{1,0},{2,3},{3,2},{4,5},{5,4},{6,7},{7,6},{8,9},{9,8},{10,11... | collective-permute-start | bytes 786440 | tf_op jit(solution)/shard_map/ppermute | solution.py:46
  41.3 2.1 %collective-permute-start.13 = (bf16[512,256]{1,0:T(8,128)(2,1)S(1)}, bf16[512,256]{1,0:T(8,128)(2,1)S(1)}, u32[]{:S(2)}, u32[]{:S(2)}) collective-permute-start(bf16[512,256]{1,0:T(8,128)(2,1)S(1)} %collective-permute-done.8.refs_3_), channel_id=1, source_target_pairs={{0,1},{1,0},{2,3},{3,2},{4,5},{5,4},{6,7},{7,6},{8,9},{9,8},{10,11... | collective-permute-start | bytes 786440 | tf_op jit(solution)/shard_map/ppermute | solution.py:46
  44.5 11.2 %copy-start = (bf16[128,1024]{1,0:T(8,128)(2,1)S(1)}, bf16[128,1024]{1,0:T(8,128)(2,1)}, u32[]{:S(2)}) copy-start(bf16[128,1024]{1,0:T(8,128)(2,1)} %query.1) | copy-start | bytes 786436
  44.5 11.2 %copy-start.1 = (bf16[128,1024]{1,0:T(8,128)(2,1)S(1)}, bf16[128,1024]{1,0:T(8,128)(2,1)}, u32[]{:S(2)}) copy-start(bf16[128,1024]{1,0:T(8,128)(2,1)} %grad_out.1) | copy-start | bytes 786436
  44.5 8.4 %collective-permute-start.15 = (bf16[1024,128]{1,0:T(8,128)(2,1)S(1)}, bf16[1024,128]{1,0:T(8,128)(2,1)S(1)}, u32[]{:S(2)}, u32[]{:S(2)}) collective-permute-start(bf16[1024,128]{1,0:T(8,128)(2,1)S(1)} %pick_tail.2), channel_id=1, source_target_pairs={{0,64},{64,128},{128,192},{192,0},{1,65},{65,129},{129,193},{193,1... | collective-permute-start | bytes 786440 | tf_op jit(solution)/shard_map/ppermute | solution.py:440
  52.9 2.7 %collective-permute-start.16 = (bf16[1024,128]{1,0:T(8,128)(2,1)S(1)}, bf16[1024,128]{1,0:T(8,128)(2,1)S(1)}, u32[]{:S(2)}, u32[]{:S(2)}) collective-permute-start(bf16[1024,128]{1,0:T(8,128)(2,1)S(1)} %collective-permute-done.15.refs_10_), channel_id=1, source_target_pairs={{0,1},{1,0},{2,3},{3,2},{4,5},{5,4},{6,7},{7,6},{8,9},{9,8},{10,11... | collective-permute-start | bytes 786440 | tf_op jit(solution)/shard_map/ppermute | solution.py:46
  53.9 9.3 %collective-permute-start.18 = (bf16[1024,128]{1,0:T(8,128)(2,1)S(1)}, bf16[1024,128]{1,0:T(8,128)(2,1)S(1)}, u32[]{:S(2)}, u32[]{:S(2)}) collective-permute-start(bf16[1024,128]{1,0:T(8,128)(2,1)S(1)} %pick_tail.3), channel_id=1, source_target_pairs={{0,64},{64,128},{128,192},{192,0},{1,65},{65,129},{129,193},{193,1... | collective-permute-start | bytes 786440 | tf_op jit(solution)/shard_map/ppermute | solution.py:440
  62.9 1.6 %collective-permute-start.17 = (bf16[1024,128]{1,0:T(8,128)(2,1)S(1)}, bf16[1024,128]{1,0:T(8,128)(2,1)S(1)}, u32[]{:S(2)}, u32[]{:S(2)}) collective-permute-start(bf16[1024,128]{1,0:T(8,128)(2,1)S(1)} %get-tuple-element.47), channel_id=1, source_target_pairs={{0,1},{1,0},{2,3},{3,2},{4,5},{5,4},{6,7},{7,6},{8,9},{9,8},{10,11... | collective-permute-start | bytes 786440 | tf_op jit(solution)/shard_map/ppermute | solution.py:46
  63.2 1.8 %collective-permute-start.19 = (bf16[1024,128]{1,0:T(8,128)(2,1)S(1)}, bf16[1024,128]{1,0:T(8,128)(2,1)S(1)}, u32[]{:S(2)}, u32[]{:S(2)}) collective-permute-start(bf16[1024,128]{1,0:T(8,128)(2,1)S(1)} %collective-permute-done.18.refs_10_), channel_id=1, source_target_pairs={{0,1},{1,0},{2,3},{3,2},{4,5},{5,4},{6,7},{7,6},{8,9},{9,8},{10,11... | collective-permute-start | bytes 786440 | tf_op jit(solution)/shard_map/ppermute | solution.py:46
  64.6 9.7 %collective-permute-start.20 = (bf16[1024,128]{1,0:T(8,128)(2,1)S(1)}, bf16[1024,128]{1,0:T(8,128)(2,1)S(1)}, u32[]{:S(2)}, u32[]{:S(2)}) collective-permute-start(bf16[1024,128]{1,0:T(8,128)(2,1)S(1)} %add_convert_fusion.5), channel_id=1, source_target_pairs={{64,0},{128,64},{192,128},{0,192},{65,1},{129,65},{193,129},{1,193... | collective-permute-start | bytes 786440 | tf_op jit(solution)/shard_map/ppermute | solution.py:446
  74.3 1.5 %collective-permute-start.21 = (bf16[1024,128]{1,0:T(8,128)(2,1)S(1)}, bf16[1024,128]{1,0:T(8,128)(2,1)S(1)}, u32[]{:S(2)}, u32[]{:S(2)}) collective-permute-start(bf16[1024,128]{1,0:T(8,128)(2,1)S(1)} %get-tuple-element.59), channel_id=1, source_target_pairs={{0,1},{1,0},{2,3},{3,2},{4,5},{5,4},{6,7},{7,6},{8,9},{9,8},{10,11... | collective-permute-start | bytes 786440 | tf_op jit(solution)/shard_map/ppermute | solution.py:46
  75.9 9.6 %collective-permute-start.22 = (bf16[1024,128]{1,0:T(8,128)(2,1)S(1)}, bf16[1024,128]{1,0:T(8,128)(2,1)S(1)}, u32[]{:S(2)}, u32[]{:S(2)}) collective-permute-start(bf16[1024,128]{1,0:T(8,128)(2,1)S(1)} %add_convert_fusion.4), channel_id=1, source_target_pairs={{64,0},{128,64},{192,128},{0,192},{65,1},{129,65},{193,129},{1,193... | collective-permute-start | bytes 786440 | tf_op jit(solution)/shard_map/ppermute | solution.py:450
  87.4 2.0 %collective-permute-start.24 = (bf16[1024,256]{1,0:T(8,128)(2,1)S(1)}, bf16[1024,256]{1,0:T(8,128)(2,1)S(1)}, u32[]{:S(2)}, u32[]{:S(2)}) collective-permute-start(bf16[1024,256]{1,0:T(8,128)(2,1)S(1)} %get-tuple-element.64), channel_id=1, source_target_pairs={{0,1},{1,0},{2,3},{3,2},{4,5},{5,4},{6,7},{7,6},{8,9},{9,8},{10,11... | collective-permute-start | bytes 1572872 | tf_op jit(solution)/shard_map/ppermute | solution.py:46
  87.5 3.2 %collective-permute-start.26 = (bf16[1024,256]{1,0:T(8,128)(2,1)S(1)}, bf16[1024,256]{1,0:T(8,128)(2,1)S(1)}, u32[]{:S(2)}, u32[]{:S(2)}) collective-permute-start(bf16[1024,256]{1,0:T(8,128)(2,1)S(1)} %get-tuple-element.66), channel_id=1, source_target_pairs={{0,1},{1,0},{2,3},{3,2},{4,5},{5,4},{6,7},{7,6},{8,9},{9,8},{10,11... | collective-permute-start | bytes 1572872 | tf_op jit(solution)/shard_map/ppermute | solution.py:46
  88.0 3.9 %collective-permute-start.28 = (bf16[512,256]{1,0:T(8,128)(2,1)S(1)}, bf16[512,256]{1,0:T(8,128)(2,1)S(1)}, u32[]{:S(2)}, u32[]{:S(2)}) collective-permute-start(bf16[512,256]{1,0:T(8,128)(2,1)S(1)} %get-tuple-element.68), channel_id=1, source_target_pairs={{0,1},{1,0},{2,3},{3,2},{4,5},{5,4},{6,7},{7,6},{8,9},{9,8},{10,11... | collective-permute-start | bytes 786440 | tf_op jit(solution)/shard_map/ppermute | solution.py:46
  88.3 5.9 %collective-permute-start.23 = (bf16[1024,256]{1,0:T(8,128)(2,1)S(1)}, bf16[1024,256]{1,0:T(8,128)(2,1)S(1)}, u32[]{:S(2)}, u32[]{:S(2)}) collective-permute-start(bf16[1024,256]{1,0:T(8,128)(2,1)S(1)} %get-tuple-element.62), channel_id=1, source_target_pairs={{0,1},{1,0},{2,3},{3,2},{4,5},{5,4},{6,7},{7,6},{8,9},{9,8},{10,11... | collective-permute-start | bytes 1572872 | tf_op jit(solution)/shard_map/ppermute | solution.py:46
  89.5 14.0 %collective-permute-start.25 = (bf16[1024,256]{1,0:T(8,128)(2,1)S(1)}, bf16[1024,256]{1,0:T(8,128)(2,1)S(1)}, u32[]{:S(2)}, u32[]{:S(2)}) collective-permute-start(bf16[1024,256]{1,0:T(8,128)(2,1)S(1)} %add_convert_fusion.1), channel_id=1, source_target_pairs={{0,6},{1,7},{2,0},{3,1},{4,2},{5,3},{6,4},{7,5},{8,14},{9,15},{10,... | collective-permute-start | bytes 1572872 | tf_op jit(solution)/shard_map/ppermute | solution.py:46
  90.8 15.0 %collective-permute-start.27 = (bf16[1024,256]{1,0:T(8,128)(2,1)S(1)}, bf16[1024,256]{1,0:T(8,128)(2,1)S(1)}, u32[]{:S(2)}, u32[]{:S(2)}) collective-permute-start(bf16[1024,256]{1,0:T(8,128)(2,1)S(1)} %add_convert_fusion), channel_id=1, source_target_pairs={{0,2},{1,3},{2,4},{3,5},{4,6},{5,7},{6,0},{7,1},{8,10},{9,11},{10,... | collective-permute-start | bytes 1572872 | tf_op jit(solution)/shard_map/ppermute | solution.py:46
  91.9 1.5 %collective-permute-start.30 = (bf16[512,256]{1,0:T(8,128)(2,1)S(1)}, bf16[512,256]{1,0:T(8,128)(2,1)S(1)}, u32[]{:S(2)}, u32[]{:S(2)}) collective-permute-start(bf16[512,256]{1,0:T(8,128)(2,1)S(1)} %get-tuple-element.70), channel_id=1, source_target_pairs={{0,1},{1,0},{2,3},{3,2},{4,5},{5,4},{6,7},{7,6},{8,9},{9,8},{10,11... | collective-permute-start | bytes 786440 | tf_op jit(solution)/shard_map/ppermute | solution.py:46
  91.9 14.1 %collective-permute-start.29 = (bf16[512,256]{1,0:T(8,128)(2,1)S(1)}, bf16[512,256]{1,0:T(8,128)(2,1)S(1)}, u32[]{:S(2)}, u32[]{:S(2)}) collective-permute-start(bf16[512,256]{1,0:T(8,128)(2,1)S(1)} %add_convert_fusion.3), channel_id=1, source_target_pairs={{0,56},{1,57},{2,58},{3,59},{4,60},{5,61},{6,62},{7,63},{8,0},{9,1... | collective-permute-start | bytes 786440 | tf_op jit(solution)/shard_map/ppermute | solution.py:46
  93.5 12.6 %collective-permute-start.31 = (bf16[512,256]{1,0:T(8,128)(2,1)S(1)}, bf16[512,256]{1,0:T(8,128)(2,1)S(1)}, u32[]{:S(2)}, u32[]{:S(2)}) collective-permute-start(bf16[512,256]{1,0:T(8,128)(2,1)S(1)} %add_convert_fusion.2), channel_id=1, source_target_pairs={{0,8},{1,9},{2,10},{3,11},{4,12},{5,13},{6,14},{7,15},{8,16},{9,17... | collective-permute-start | bytes 786440 | tf_op jit(solution)/shard_map/ppermute | solution.py:46
  106.2 8.5 %collective-permute-start.32 = (bf16[384,256]{1,0:T(8,128)(2,1)S(1)}, bf16[384,256]{1,0:T(8,128)(2,1)S(1)}, u32[]{:S(2)}, u32[]{:S(2)}) collective-permute-start(bf16[384,256]{1,0:T(8,128)(2,1)S(1)} %pad_maximum_fusion.1), channel_id=1, source_target_pairs={{0,48},{1,17},{2,50},{3,19},{4,52},{5,21},{6,54},{7,23},{8,56},{9,... | collective-permute-start | bytes 589832 | tf_op jit(solution)/shard_map/ppermute | solution.py:46
  107.5 10.8 %collective-permute-start.35 = (bf16[256,256]{1,0:T(8,128)(2,1)S(1)}, bf16[256,256]{1,0:T(8,128)(2,1)S(1)}, u32[]{:S(2)}, u32[]{:S(2)}) collective-permute-start(bf16[256,256]{1,0:T(8,128)(2,1)S(1)} %slice.79), channel_id=1, source_target_pairs={{0,44},{1,13},{2,46},{3,15},{4,40},{5,9},{6,42},{7,11},{8,52},{9,2... | collective-permute-start | bytes 393224 | tf_op jit(solution)/shard_map/ppermute | solution.py:46
  109.2 10.5 %collective-permute-start.34 = (bf16[256,256]{1,0:T(8,128)(2,1)S(1)}, bf16[256,256]{1,0:T(8,128)(2,1)S(1)}, u32[]{:S(2)}, u32[]{:S(2)}) collective-permute-start(bf16[256,256]{1,0:T(8,128)(2,1)S(1)} %slice.77), channel_id=1, source_target_pairs={{0,60},{1,29},{2,62},{3,31},{4,56},{5,25},{6,58},{7,27},{8,4},{9,3... | collective-permute-start | bytes 393224 | tf_op jit(solution)/shard_map/ppermute | solution.py:46
  114.8 6.1 %collective-permute-start.33 = (bf16[128,256]{1,0:T(8,128)(2,1)S(1)}, bf16[128,256]{1,0:T(8,128)(2,1)S(1)}, u32[]{:S(2)}, u32[]{:S(2)}) collective-permute-start(bf16[128,256]{1,0:T(8,128)(2,1)S(1)} %slice.75), channel_id=1, source_target_pairs={{0,48},{1,17},{2,50},{3,19},{4,52},{5,21},{6,54},{7,23},{8,56},{9,... | collective-permute-start | bytes 196616 | tf_op jit(solution)/shard_map/ppermute | solution.py:46
  119.7 1.7 %collective-permute-start.36 = (bf16[128,256]{1,0:T(8,128)(2,1)S(1)}, bf16[128,256]{1,0:T(8,128)(2,1)S(1)}, u32[]{:S(2)}, u32[]{:S(2)}) collective-permute-start(bf16[128,256]{1,0:T(8,128)(2,1)S(1)} %add_convert_fusion.6), channel_id=1, source_target_pairs={{0,1},{1,0},{2,3},{3,2},{4,5},{5,4},{6,7},{7,6},{8,9},{9,8},{10,11... | collective-permute-start | bytes 196616 | tf_op jit(solution)/shard_map/ppermute | solution.py:46
